TPU v7x, 512 devices: a whole 4x8x8 slice. The times are simulated.
512 devices in a mesh: dp: 8 (over y_hi, core), view: 8 (over z), tm: 8 (over x, y_lo).
Axes of the slice: x: 4, y: 8 (y_hi: 4, y_lo: 2; y = y_hi * 2 + y_lo), z: 8, core: 2. Of those that a mesh axis runs over, the one named last changes fastest.
Arguments:
- tokens: bfloat16 [8, 8, 1024, 1024], P('dp', 'view', 'tm'), may hold values from -24 to 24
- cotangent: bfloat16 [8, 8, 1024, 1024], P('dp', 'view', 'tm'), may hold values from -6 to 6
- w_query: bfloat16 [1024, 512], P(None, 'tm'), may hold values from -0.1875 to 0.1875
- w_key: bfloat16 [1024, 512], P(None, 'tm'), may hold values from -0.1875 to 0.1875
- w_value: bfloat16 [1024, 512], P(None, 'tm'), may hold values from -0.1875 to 0.1875
- w_out: bfloat16 [512, 1024], P('tm'), may hold values from -0.25 to 0.25
- masks: int32 [4, 8, 8], replicated, may hold values from 0 to 1, as said below
- rig_ids: int32 [8], P('dp'), may hold values from 0 to 3
Outputs:
- attended: bfloat16 [8, 8, 1024, 1024], P('dp', 'view', 'tm')
- grad_tokens: bfloat16 [8, 8, 1024, 1024], P('dp', 'view', 'tm')
- grad_query: float32 [1024, 512], P(None, 'tm')
- grad_key: float32 [1024, 512], P(None, 'tm')
- grad_value: float32 [1024, 512], P(None, 'tm')
- grad_out: float32 [512, 1024], P('tm')
Inputs may be any that keep to these rules, and one draw needn't show every extreme that they name: `masks`: tile i of a time span is the 128 tokens of camera i // 1 that start at position (i % 1) * 128 of the span (with one tile a camera, tile i is the whole span of camera i); every query tile of every rig lists 1 to 4 key tiles, and every rig has a query tile that lists exactly 4.
All inputs are finite; a program needn't handle non-finite values.
Results may differ from a plain program's by a relative error of at most 0.02.
The roundings to bfloat16 on the way count: a program that leaves them out, or rounds other values in their place, can miss the bound.
Values may be sent and summed in bfloat16 or wider, within the bound.
A program may use at most 64 MiB of HBM per device.

v0:
```python
import jax
import jax.numpy as jnp
from jax import lax
from jax.sharding import PartitionSpec as P

HEADS = 8


def expand_tiles(tile_grid, tile_size):
    grid_rows, grid_cols = tile_grid.shape
    spread = jnp.broadcast_to(
        tile_grid[:, None, :, None], (grid_rows, tile_size, grid_cols, tile_size)
    )
    return spread.reshape(grid_rows * tile_size, grid_cols * tile_size) == 1


def masked_softmax(scores, allowed):
    scores = jnp.where(allowed, scores, -1e30)
    highest = jnp.max(scores, axis=-1, keepdims=True)
    weights = jnp.where(allowed, jnp.exp(scores - highest), 0.0)
    return weights / jnp.sum(weights, axis=-1, keepdims=True)


def dense_attention(query_rows, key_all, value_all, grad_attn, mask_rows, tile_size):
    count, inner = query_rows.shape
    total = key_all.shape[0]
    depth = inner // HEADS
    factor = depth ** (-0.5)
    allowed = expand_tiles(mask_rows, tile_size)[None]
    query_heads = query_rows.reshape(count, HEADS, depth)
    key_heads = key_all.reshape(total, HEADS, depth)
    value_heads = value_all.reshape(total, HEADS, depth)
    scores = (
        jnp.einsum("qhe,khe->hqk", query_heads, key_heads, preferred_element_type=jnp.float32)
        * factor
    )
    probs_full = masked_softmax(scores, allowed)
    probs_half = probs_full.astype(jnp.bfloat16)
    attn_rows = jnp.einsum(
        "hqk,khe->qhe", probs_half, value_heads, preferred_element_type=jnp.float32
    )
    attn_rows = attn_rows.reshape(count, inner).astype(jnp.bfloat16)
    grad_heads = grad_attn.reshape(count, HEADS, depth)
    grad_probs = jnp.einsum(
        "qhe,khe->hqk", grad_heads, value_heads, preferred_element_type=jnp.float32
    )
    row_terms = jnp.sum(
        grad_heads.astype(jnp.float32) * attn_rows.reshape(count, HEADS, depth).astype(jnp.float32),
        axis=-1,
    ).T
    grad_scores = (probs_full * (grad_probs - row_terms[:, :, None]) * factor).astype(jnp.bfloat16)
    grad_query = jnp.einsum(
        "hqk,khe->qhe", grad_scores, key_heads, preferred_element_type=jnp.float32
    )
    grad_query = grad_query.reshape(count, inner).astype(jnp.bfloat16)
    key_terms = jnp.einsum(
        "hqk,qhe->khe", grad_scores, query_heads, preferred_element_type=jnp.float32
    ).reshape(total, inner)
    value_terms = jnp.einsum(
        "hqk,qhe->khe", probs_half, grad_heads, preferred_element_type=jnp.float32
    ).reshape(total, inner)
    return (attn_rows, grad_query, key_terms, value_terms)


def shards(tokens, cotangent, w_query, w_key, w_value, w_out, masks, rig_ids):
    count, width = (tokens.shape[2], tokens.shape[3])
    tok_rows = tokens.reshape(count, width)
    cot_rows = cotangent.reshape(count, width)
    full_query, full_key, full_value, full_out = (
        lax.all_gather(w_query, "tm", axis=1, tiled=True),
        lax.all_gather(w_key, "tm", axis=1, tiled=True),
        lax.all_gather(w_value, "tm", axis=1, tiled=True),
        lax.all_gather(w_out, "tm", axis=0, tiled=True),
    )
    query_rows = jnp.dot(tok_rows, full_query, preferred_element_type=jnp.float32).astype(
        jnp.bfloat16
    )
    key_rows = jnp.dot(tok_rows, full_key, preferred_element_type=jnp.float32).astype(jnp.bfloat16)
    value_rows = jnp.dot(tok_rows, full_value, preferred_element_type=jnp.float32).astype(
        jnp.bfloat16
    )
    key_all, value_all = (
        lax.all_gather(key_rows, "view", axis=0, tiled=True),
        lax.all_gather(value_rows, "view", axis=0, tiled=True),
    )
    grad_attn = jnp.dot(cot_rows, full_out.T, preferred_element_type=jnp.float32).astype(
        jnp.bfloat16
    )
    tile_count = masks.shape[1]
    query_tiles = tile_count // lax.axis_size("view")
    tile_size = count // query_tiles
    rig_table = lax.dynamic_index_in_dim(masks, rig_ids[0], 0, keepdims=False)
    mask_rows = lax.dynamic_slice_in_dim(
        rig_table, lax.axis_index("view") * query_tiles, query_tiles, 0
    )
    attn_rows, grad_query, key_terms, value_terms = dense_attention(
        query_rows, key_all, value_all, grad_attn, mask_rows, tile_size
    )
    attended = jnp.dot(attn_rows, full_out, preferred_element_type=jnp.float32).astype(jnp.bfloat16)
    key_total, value_total = (
        lax.psum_scatter(
            key_terms.astype(jnp.bfloat16), "view", scatter_dimension=0, tiled=True
        ).astype(jnp.float32),
        lax.psum_scatter(
            value_terms.astype(jnp.bfloat16), "view", scatter_dimension=0, tiled=True
        ).astype(jnp.float32),
    )
    grad_key = key_total.astype(jnp.bfloat16)
    grad_value = value_total.astype(jnp.bfloat16)
    grad_rows = (
        jnp.dot(grad_query, full_query.T, preferred_element_type=jnp.float32)
        + jnp.dot(grad_key, full_key.T, preferred_element_type=jnp.float32)
        + jnp.dot(grad_value, full_value.T, preferred_element_type=jnp.float32)
    ).astype(jnp.bfloat16)
    tok_all, cot_all = (
        lax.all_gather(tok_rows, "tm", axis=0, tiled=True),
        lax.all_gather(cot_rows, "tm", axis=0, tiled=True),
    )
    query_cols, key_cols, value_cols, attn_cols = (
        lax.all_to_all(grad_query, "tm", split_axis=1, concat_axis=0, tiled=True),
        lax.all_to_all(grad_key, "tm", split_axis=1, concat_axis=0, tiled=True),
        lax.all_to_all(grad_value, "tm", split_axis=1, concat_axis=0, tiled=True),
        lax.all_to_all(attn_rows, "tm", split_axis=1, concat_axis=0, tiled=True),
    )
    out_local = jnp.dot(attn_cols.T, cot_all, preferred_element_type=jnp.float32)
    query_local = jnp.dot(tok_all.T, query_cols, preferred_element_type=jnp.float32)
    key_local = jnp.dot(tok_all.T, key_cols, preferred_element_type=jnp.float32)
    value_local = jnp.dot(tok_all.T, value_cols, preferred_element_type=jnp.float32)
    grad_wq, grad_wk, grad_wv, grad_wo = lax.psum(
        (query_local, key_local, value_local, out_local), ("dp", "view")
    )
    return (
        attended.reshape(tokens.shape),
        grad_rows.reshape(tokens.shape),
        grad_wq,
        grad_wk,
        grad_wv,
        grad_wo,
    )


def solution(mesh):
    return jax.shard_map(
        shards,
        mesh=mesh,
        in_specs=(
            P("dp", "view", "tm", None),
            P("dp", "view", "tm", None),
            P(None, "tm"),
            P(None, "tm"),
            P(None, "tm"),
            P("tm", None),
            P(),
            P("dp"),
        ),
        out_specs=(
            P("dp", "view", "tm", None),
            P("dp", "view", "tm", None),
            P(None, "tm"),
            P(None, "tm"),
            P(None, "tm"),
            P("tm", None),
        ),
        check_vma=False,
    )
```

profile of v0, /device:TPU:1, one launch (start us, length us, event | category | flops | bytes accessed | tf_op | source)
XLA Modules:
  0.0 1073.3 jit_solution(15636634996484448013)
XLA Ops:
  10.0 46.6 %all-gather.11.cloned.1.call-done = bf16[1024,512]{0,1:T(8,128)(2,1)} async-done(((bf16[1024,64]{0,1:T(8,128)(2,1)}), bf16[1024,512]{0,1:T(8,128)(2,1)}) %all-gather.11.cloned.1.call-update) | async-done | bytes 1048592 | tf_op jit(solution)/shard_map/all_gather | solution.py:72
  56.6 2.5 convolution_convert_fusion.8
  59.2 44.3 %all-gather.17.cloned.1.call-done = bf16[1024,512]{0,1:T(8,128)(2,1)} async-done(((bf16[1024,64]{0,1:T(8,128)(2,1)}), bf16[1024,512]{0,1:T(8,128)(2,1)}) %all-gather.17.cloned.1.call-update) | async-done | bytes 1048592 | tf_op jit(solution)/shard_map/all_gather | solution.py:71
  103.4 2.4 convolution_convert_fusion.6
  108.1 42.2 %all-gather.21.cloned.1.call-done = bf16[512,1024]{1,0:T(8,128)(2,1)} async-done(((bf16[64,1024]{1,0:T(8,128)(2,1)}), bf16[512,1024]{1,0:T(8,128)(2,1)}) %all-gather.21.cloned.1.call-update) | async-done | bytes 1048592 | tf_op jit(solution)/shard_map/all_gather | solution.py:73
  150.3 1.7 convolution_convert_fusion.4
  152.1 44.8 %all-gather.15.cloned.1.call-done = bf16[1024,512]{0,1:T(8,128)(2,1)} async-done(((bf16[1024,64]{0,1:T(8,128)(2,1)}), bf16[1024,512]{0,1:T(8,128)(2,1)}) %all-gather.15.cloned.1.call-update) | async-done | bytes 1048592 | tf_op jit(solution)/shard_map/all_gather | solution.py:70
  196.9 1.7 convolution_convert_fusion.7
  198.8 42.0 %all-gather.13.cloned.1.call-done = bf16[1024,512]{1,0:T(8,128)(2,1)} async-done(((bf16[128,512]{1,0:T(8,128)(2,1)}), bf16[1024,512]{1,0:T(8,128)(2,1)}) %all-gather.13.cloned.1.call-update) | async-done | bytes 1048592 | tf_op jit(solution)/shard_map/all_gather | solution.py:84
  240.8 2.3 copy.35
  243.1 40.6 %all-gather.19.cloned.1.call-done = bf16[1024,512]{1,0:T(8,128)(2,1)} async-done(((bf16[128,512]{1,0:T(8,128)(2,1)}), bf16[1024,512]{1,0:T(8,128)(2,1)}) %all-gather.19.cloned.1.call-update) | async-done | bytes 1048592 | tf_op jit(solution)/shard_map/all_gather | solution.py:83
  285.1 3.7 fusion.42
  288.8 2.9 fusion.13
  297.0 2.3 copy.43
  301.4 2.5 copy.45
  304.8 11.9 %all_to_all.70 = bf16[128,8,64]{0,2,1:T(8,128)(2,1)S(1)} all-to-all(bf16[128,8,64]{0,2,1:T(8,128)(2,1)S(1)} %bitcast.131), channel_id=1, replica_groups=mesh['dp'=8,'view'=8,'tm'=8] {'tm'}, dimensions={1} | all-to-all | bytes 262144 | tf_op jit(solution)/shard_map/all_to_all | solution.py:120
  316.7 3.4 all-to-all-start.3
  320.0 28.4 %all-gather.23.cloned.1.call-done = bf16[1,1,1024,1024]{3,2,1,0:T(8,128)(2,1)} async-done(((bf16[1,1,128,1024]{3,2,1,0:T(8,128)(2,1)}), bf16[1,1,1024,1024]{3,2,1,0:T(8,128)(2,1)}) %all-gather.23.cloned.1.call-update) | async-done | bytes 2097168 | tf_op jit(solution)/shard_map/all_gather | solution.py:116
  348.4 2.8 fusion.16
  351.2 37.1 %reduce-scatter.7.cloned.1.call-done = bf16[128,512]{1,0:T(8,128)(2,1)} async-done(((bf16[1024,512]{1,0:T(8,128)(2,1)}), bf16[128,512]{1,0:T(8,128)(2,1)}) %reduce-scatter.7.cloned.1.call-update) | async-done | bytes 131088
  390.0 4.9 all-to-all-start.1
  394.9 55.6 %all-gather.25.cloned.1.call-done = bf16[1,1,1024,1024]{3,2,1,0:T(8,128)(2,1)} async-done(((bf16[1,1,128,1024]{3,2,1,0:T(8,128)(2,1)}), bf16[1,1,1024,1024]{3,2,1,0:T(8,128)(2,1)}) %all-gather.25.cloned.1.call-update) | async-done | bytes 2097168 | tf_op jit(solution)/shard_map/all_gather | solution.py:117
  450.4 2.8 fusion.2
  453.2 36.5 %reduce-scatter.9.cloned.1.call-done = bf16[128,512]{1,0:T(8,128)(2,1)} async-done(((bf16[1024,512]{1,0:T(8,128)(2,1)}), bf16[128,512]{1,0:T(8,128)(2,1)}) %reduce-scatter.9.cloned.1.call-update) | async-done | bytes 131088
  491.4 4.9 all-to-all-start.2
  497.6 4.3 all-to-all-done.2
  503.1 2.1 fusion.15
  507.4 552.6 %all-reduce.3.cloned.1.call-done = (f32[1024,64]{0,1:T(8,128)}, f32[1024,64]{0,1:T(8,128)}, f32[1024,64]{0,1:T(8,128)}, f32[64,1024]{1,0:T(8,128)}) async-done(((f32[1024,64]{0,1:T(8,128)}, f32[1024,64]{0,1:T(8,128)}, f32[1024,64]{0,1:T(8,128)}, f32[64,1024]{1,0:T(8,128)}), (f32[1024,64]{0,1:T(8,128)}, f32[1024,64]{0,1:T(8,128)}, f32[1024,64]{0,1:T(8,128)}, ...) | async-done | bytes 1048592 | tf_op jit(solution)/shard_map/psum | solution.py:129
  1060.1 1.7 copy.72
  1061.7 1.7 copy.73
  1063.4 1.7 copy.74
  1065.1 1.7 copy.75
  (69 shorter events, 22.4 us)
Async XLA Ops:
  7.2 96.3 %copy-start.9 = (bf16[1,1,128,1024]{3,2,1,0:T(8,128)(2,1)S(1)}, bf16[1,1,128,1024]{3,2,1,0:T(8,128)(2,1)}, u32[]{:S(2)}) copy-start(bf16[1,1,128,1024]{3,2,1,0:T(8,128)(2,1)} %param.8) | copy-start | bytes 786436
  7.2 143.1 %copy-start.11 = (bf16[1,1,128,1024]{3,2,1,0:T(8,128)(2,1)S(1)}, bf16[1,1,128,1024]{3,2,1,0:T(8,128)(2,1)}, u32[]{:S(2)}) copy-start(bf16[1,1,128,1024]{3,2,1,0:T(8,128)(2,1)} %param.9) | copy-start | bytes 786436
  7.2 49.4 %all-gather.11.cloned.1.call-start = ((), (), s32[]{:S(2)}) async-start(), calls=%async_computation.6 | async-start | bytes 1179648 | tf_op jit(solution)/shard_map/all_gather | solution.py:72
  7.9 95.5 %all-gather.17.cloned.1.call-start = ((), (), s32[]{:S(2)}) async-start(), calls=%async_computation.9 | async-start | bytes 1179648 | tf_op jit(solution)/shard_map/all_gather | solution.py:71
  8.7 141.6 %all-gather.21.cloned.1.call-start = ((), (), s32[]{:S(2)}) async-start(), calls=%async_computation.11 | async-start | bytes 1179648 | tf_op jit(solution)/shard_map/all_gather | solution.py:73
  9.4 187.5 %all-gather.15.cloned.1.call-start = ((), (), s32[]{:S(2)}) async-start(), calls=%async_computation.8 | async-start | bytes 1179648 | tf_op jit(solution)/shard_map/all_gather | solution.py:70
  10.0 230.8 %all-gather.13.cloned.1.call-start = ((), (), s32[]{:S(2)}) async-start(), calls=%async_computation.7 | async-start | bytes 1179648 | tf_op jit(solution)/shard_map/all_gather | solution.py:84
  59.1 137.9 %copy-start.10 = (bf16[1,1,128,1024]{3,2,1,0:T(8,128)(2,1)S(1)}, bf16[1,1,128,1024]{3,2,1,0:T(8,128)(2,1)}, u32[]{:S(2)}) copy-start(bf16[1,1,128,1024]{3,2,1,0:T(8,128)(2,1)} %param.8) | copy-start | bytes 786436
  59.1 224.5 %all-gather.19.cloned.1.call-start = ((), (), s32[]{:S(2)}) async-start(), calls=%async_computation.10 | async-start | bytes 1179648 | tf_op jit(solution)/shard_map/all_gather | solution.py:83
  105.8 242.6 %all-gather.23.cloned.1.call-start = ((), (), s32[]{:S(2)}) async-start(), calls=%async_computation.12 | async-start | bytes 2359296 | tf_op jit(solution)/shard_map/all_gather | solution.py:116
  106.6 281.7 %reduce-scatter.7.cloned.1.call-start = ((), (), s32[]{:S(2)}) async-start(), calls=%async_computation.14 | async-start | bytes 1179648
  288.8 2.9 copy-start.8
  288.8 4.4 copy-start.3
  294.2 1.4 copy-start.1
  299.2 151.2 %all-gather.25.cloned.1.call-start = ((), (), s32[]{:S(2)}) async-start(), calls=%async_computation.13 | async-start | bytes 2359296 | tf_op jit(solution)/shard_map/all_gather | solution.py:117
  300.0 189.8 %reduce-scatter.9.cloned.1.call-start = ((), (), s32[]{:S(2)}) async-start(), calls=%async_computation.15 | async-start | bytes 1179648
  301.4 2.5 copy-start.2
  316.7 73.3 %all-to-all-start.3 = ((bf16[128,8,64]{0,2,1:T(8,128)(2,1)}), bf16[128,8,64]{0,2,1:T(8,128)(2,1)S(1)}, u32[]{:S(2)}, u32[]{:S(2)}) async-start(bf16[128,8,64]{0,2,1:T(8,128)(2,1)} %bitcast.7), calls=%async_computation.3 | async-start | bytes 262144 | tf_op jit(solution)/shard_map/all_to_all | solution.py:123
  351.2 145.2 %copy-start = (bf16[1,1,1024,1024]{3,2,1,0:T(8,128)(2,1)S(1)}, bf16[1,1,1024,1024]{3,2,1,0:T(8,128)(2,1)}, u32[]{:S(2)}) copy-start(bf16[1,1,1024,1024]{3,2,1,0:T(8,128)(2,1)} %all-gather.23.cloned.1.call-done) | copy-start | bytes 6291460
  390.0 101.4 %all-to-all-start.1 = ((bf16[128,8,64]{0,2,1:T(8,128)(2,1)}), bf16[128,8,64]{0,2,1:T(8,128)(2,1)S(1)}, u32[]{:S(2)}, u32[]{:S(2)}) async-start(bf16[128,8,64]{0,2,1:T(8,128)(2,1)} %bitcast.23), calls=%async_computation.1 | async-start | bytes 262144 | tf_op jit(solution)/shard_map/all_to_all | solution.py:121
  491.4 10.4 all-to-all-start.2
  496.3 563.7 %all-reduce.3.cloned.1.call-start = ((), (), s32[]{:S(2)}) async-start(), calls=%async_computation.16 | async-start | bytes 2097152 | tf_op jit(solution)/shard_map/psum | solution.py:129
  497.6 5.5 copy-start.5
  503.0 2.1 copy-start.7
  503.1 2.5 copy-start.4
  503.1 2.5 copy-start.12
  505.2 1.2 copy-start.6
  505.2 1.2 copy-start.13
Sparse Core Ops, SparseCore 0:
  10.1 46.4 all-gather.10
  58.7 44.6 all-gather.16
  105.5 44.6 all-gather.20
  152.2 44.6 all-gather.14
  199.4 41.3 all-gather.12
  243.3 40.2 all-gather.18
  285.7 62.6 all-gather.22
  351.2 37.0 reduce-scatter.6
  390.4 59.9 all-gather.24
  453.1 36.6 reduce-scatter.8
  503.2 556.8 all-reduce.2
where the time goes:
time: 1080 us; the launch traced here: 1070 us
  waiting for transfers between devices  979 us (91%)
  matrix products  29.7 us (3%)
  local copies, waits for them, and re-layouts  20.7 us (2%)
  between operations  14.7 us (1%)
  starting transfers between devices  13.6 us (1%)
  blocking collectives  11.9 us (1%)
    psum x1, waiting for transfers between devices, shards(): lax.psum((query_local, key_local, value_local, out_local), ('dp', 'view'))  553 us
    unnamed x13, waiting for transfers between devices  77.7 us
    all_gather x1, waiting for transfers between devices, shards(): lax.all_gather(cot_rows, 'tm', axis=0, tiled=True)  55.6 us
    all_gather x1, waiting for transfers between devices, shards(): lax.all_gather(w_value, 'tm', axis=1, tiled=True)  46.6 us
    all_gather x1, waiting for transfers between devices, shards(): lax.all_gather(w_query, 'tm', axis=1, tiled=True)  44.8 us
    all_gather x1, waiting for transfers between devices, shards(): lax.all_gather(w_key, 'tm', axis=1, tiled=True)  44.3 us
    all_gather x1, waiting for transfers between devices, shards(): lax.all_gather(w_out, 'tm', axis=0, tiled=True)  42.2 us
    all_gather x1, waiting for transfers between devices, shards(): lax.all_gather(value_rows, 'view', axis=0, tiled=True)  42 us
  transfers between devices with their start and end apart: 14, of which 12 were waited for; matrix products, arithmetic and copies ran while one was open for 4% of the time, Pallas kernels for 0%

commit v1 on v0

v1 whole, which is shorter than its diff:
```python
import functools

import jax
import jax.numpy as jnp
from jax import lax
from jax.experimental import pallas as pl
from jax.experimental.pallas import tpu as pltpu
from jax.sharding import PartitionSpec as P

MESH = pl.DeviceIdType.MESH
BF16 = jnp.bfloat16
F32 = jnp.float32

KW, KS, KT, KC, KP, KX1, KX2, KB1, KB2, KR, KZ, KY, KF, KG = range(14)
KINDS = 14

NT = (((1,), (1,)), ((), ()))


def dot(a, b):
    return jnp.dot(a, b, preferred_element_type=F32)


def dot_nt(a, b):
    return lax.dot_general(a, b, NT, preferred_element_type=F32)


def kernel(
    n_d, n_z, n_t, depth,
    tok_ref, cot_ref, w_ref, masks_ref, rig_ref,
    att_ref, gtok_ref, g_ref,
    w_all, tok_all, cot_all, p_send, p_all, kv_t, acc, x1, x2, xa1, xa2, xb1, xb2,
    g_sum, c_send, c_recv, z_send, z_recv, y_recv, fin,
    ssem, rsem,
):
    rows, width = tok_ref.shape
    lanes = 2 * depth
    n_x = n_t // 2
    n_y = n_d // 2
    dp, z, tm = lax.axis_index("dp"), lax.axis_index("view"), lax.axis_index("tm")
    core, yh = dp % 2, dp // 2
    x, yl = tm // 2, tm % 2
    sib = dp + 1 - 2 * core

    def copy(src, dst, kind, at, **to):
        return pltpu.make_async_remote_copy(
            src_ref=src, dst_ref=dst, send_sem=ssem.at[kind, at], recv_sem=rsem.at[kind, at],
            device_id=to, device_id_type=MESH,
        )

    barrier = pltpu.get_barrier_semaphore()
    greeted = 0
    for s in range(1, n_t):
        pl.semaphore_signal(barrier, inc=1, device_id={"tm": (tm + s) % n_t}, device_id_type=MESH)
        greeted += 1
    for s in range(1, n_z):
        pl.semaphore_signal(barrier, inc=1, device_id={"view": (z + s) % n_z}, device_id_type=MESH)
        greeted += 1
    for s in range(1, n_y):
        pl.semaphore_signal(barrier, inc=1, device_id={"dp": (dp + 2 * s) % n_d}, device_id_type=MESH)
        greeted += 1
    pl.semaphore_signal(barrier, inc=1, device_id={"dp": sib}, device_id_type=MESH)
    greeted += 1
    pl.semaphore_wait(barrier, greeted)

    def offsets(step):
        g = step // 2
        dx = g + g // 2 - 2 * (g // 3) if n_x == 4 else g
        return dx, step % 2

    def peer(step):
        dx, dy = offsets(step)
        return ((x + dx) % n_x) * 2 + (yl + dy) % 2

    def source(step):
        dx, dy = offsets(step)
        return ((x - dx + n_x) % n_x) * 2 + (yl + dy) % 2

    half = width // 2
    mine = pl.ds(pl.multiple_of(core * half, half), half)
    for step in range(1, n_t):
        copy(w_ref.at[mine], w_all.at[tm, mine], KW, step, tm=peer(step)).start()
    w_all[tm] = w_ref[...]
    tok_all[tm] = tok_ref[...]
    cot_all[tm] = cot_ref[...]

    first = lax.broadcasted_iota(jnp.int32, (rows, lanes), 1) < depth

    def project(head):
        weights = w_all[head]
        by_tok = dot(tok_ref[...], weights)
        by_cot = dot(cot_ref[...], weights[:, :lanes])
        p_send[head, :, :lanes] = jnp.where(first, by_tok[:, :lanes], by_cot).astype(BF16)
        p_send[head, :, lanes:] = by_tok[:, lanes:].astype(BF16)

        @pl.when(head == z)
        def _():
            p_all[z] = p_send[head]

        @pl.when(head != z)
        def _():
            copy(p_send.at[head], p_all.at[z], KP, (head - z + n_z) % n_z, view=head).start()

    def w_part(step):
        return w_all.at[source(step), mine]

    def w_step(step, _):
        copy(w_part(step), w_part(step), KW, step, tm=peer(step)).wait_recv()
        copy(w_part(step), w_part(step), KS, step, dp=sib).start()

        @pl.when(step > 1)
        def _():
            w_other(step - 1)

        project(source(step - 1))
        return 0

    theirs = pl.ds(pl.multiple_of((1 - core) * half, half), half)

    def w_other(step):
        part = w_all.at[source(step), theirs]
        copy(part, part, KS, step, dp=sib).wait_recv()

    lax.fori_loop(1, n_t, w_step, 0)
    w_other(n_t - 1)
    project(source(n_t - 1))

    for step in range(1, n_t):
        copy(tok_ref, tok_all.at[tm], KT, step, tm=peer(step)).start()
        copy(cot_ref, cot_all.at[tm], KC, step, tm=peer(step)).start()

    for d in range(1, n_z):
        copy(p_send.at[0], p_all.at[(z - d + n_z) % n_z], KP, d, view=(z + d) % n_z).wait_recv()

    total = n_z * rows
    kv_t[...] = p_all[:, :, lanes:].reshape(total, lanes).T
    acc[...] = jnp.zeros_like(acc)
    rig = rig_ref[0]
    factor = depth ** -0.5

    def attend(cam, _):
        qd = p_all[cam, :, :lanes]
        zero = jnp.zeros_like(qd)
        block = jnp.concatenate([jnp.where(first, qd, zero), jnp.where(first, zero, qd)], axis=0)
        kv = p_all[:, :, lanes:].reshape(total, lanes)
        both = dot_nt(kv, block)
        scores = jnp.concatenate(
            [
                both[b * rows:(b + 1) * rows, :rows] * factor
                + (masks_ref[rig, cam, b] - 1).astype(F32) * 1e30
                for b in range(n_z)
            ],
            axis=0,
        )
        weights = jnp.exp(scores - jnp.max(scores, axis=0, keepdims=True))
        probs = weights * (1.0 / jnp.sum(weights, axis=0, keepdims=True))
        probs_half = probs.astype(BF16)
        attn = dot(kv_t[depth:], probs_half)
        grad_attn = qd.astype(F32).T[depth:]
        delta = jnp.sum(grad_attn * attn.astype(BF16).astype(F32), axis=0, keepdims=True)
        dscore = (probs * (both[:, rows:] - delta) * factor).astype(BF16)
        dq = dot(kv_t[:depth], dscore)
        x1[cam] = jnp.concatenate([dq, attn], axis=0).T.astype(BF16)

        @pl.when(cam == z)
        def _():
            xa1[z] = x1[cam]

        @pl.when(cam != z)
        def _():
            copy(x1.at[cam], xa1.at[z], KX1, (cam - z + n_z) % n_z, view=cam).start()

        part = dot(jnp.concatenate([dscore, probs_half], axis=1), block)
        acc[...] += part.astype(BF16).astype(F32)
        return 0

    lax.fori_loop(0, n_z, attend, 0)
    x2[...] = acc[...].astype(BF16).reshape(n_z, rows, lanes)
    for d in range(1, n_z):
        cam = (z + d) % n_z
        copy(x2.at[cam], xa2.at[z], KX2, d, view=cam).start()
    xa2[z] = x2[z]

    def hand_on(src, dst, kind, head):
        @pl.when(head == tm)
        def _():
            dst[tm] = src[head]

        @pl.when(head != tm)
        def _():
            copy(src.at[head], dst.at[tm], kind, (head - tm + n_t) % n_t, tm=head).start()

    def arrive1(d, _):
        head = (z - d + n_z) % n_z

        @pl.when(d > 0)
        def _():
            copy(xa1.at[head], xa1.at[head], KX1, d, view=head).wait_recv()

        hand_on(xa1, xb1, KB1, head)
        return 0

    def arrive2(d, _):
        head = (z - d + n_z) % n_z

        @pl.when(d > 0)
        def _():
            copy(xa2.at[head], xa2.at[head], KX2, d, view=head).wait_recv()

        hand_on(xa2, xb2, KB2, head)
        return 0

    lax.fori_loop(0, n_z, arrive1, 0)
    lax.fori_loop(0, n_z, arrive2, 0)

    for f in range(1, n_t):
        span = (tm - f + n_t) % n_t
        copy(xb1.at[span], xb1.at[span], KB1, f, tm=span).wait_recv()
        copy(xb2.at[span], xb2.at[span], KB2, f, tm=span).wait_recv()
    for step in range(1, n_t):
        span = source(step)
        copy(tok_all.at[span], tok_all.at[span], KT, step, tm=peer(step)).wait_recv()
        copy(cot_all.at[span], cot_all.at[span], KC, step, tm=peer(step)).wait_recv()

    b1 = xb1[...].reshape(n_t * rows, lanes).T
    b2 = xb2[...].reshape(n_t * rows, lanes).T
    tokens = tok_all[...].reshape(n_t * rows, width)
    cots = cot_all[...].reshape(n_t * rows, width)
    g_sum[:depth] = dot(b1[:depth], tokens)
    g_sum[depth:lanes] = dot(b1[depth:], cots)
    g_sum[lanes:] = dot(b2, tokens)

    keep = pl.ds(pl.multiple_of(core * lanes, lanes), lanes)
    give = pl.ds(pl.multiple_of((1 - core) * lanes, lanes), lanes)
    c_send[...] = g_sum[give].astype(BF16)
    core_copy = copy(c_send, c_recv, KR, 0, dp=sib)
    core_copy.start()
    core_copy.wait_recv()
    g_sum[keep] = g_sum[keep] + c_recv[...].astype(F32)
    z_send[...] = g_sum[keep].astype(BF16)

    chunk = lanes // n_z

    def rows_of(index):
        return pl.ds(pl.multiple_of(index * chunk, chunk), chunk)

    for d in range(1, n_z):
        cam = (z + d) % n_z
        copy(z_send.at[rows_of(cam)], z_recv.at[z], KZ, d, view=cam).start()

    def finish(head, sums):
        one, two = xa1[head], xa2[head]
        zero = jnp.zeros_like(one)
        left = jnp.concatenate(
            [
                jnp.concatenate([jnp.where(first, one, zero), two], axis=1),
                jnp.concatenate([jnp.where(first, zero, one), zero], axis=1),
            ],
            axis=0,
        )
        return sums + dot_nt(left, w_all[head])

    sums = lax.fori_loop(0, n_z, finish, jnp.zeros((2 * rows, width), F32))
    gtok_ref[...] = sums[:rows].astype(BF16)
    att_ref[...] = sums[rows:].astype(BF16)

    chunk_sum = z_send[rows_of(z)].astype(F32)
    for d in range(1, n_z):
        cam = (z - d + n_z) % n_z
        copy(z_recv.at[cam], z_recv.at[cam], KZ, d, view=cam).wait_recv()
        chunk_sum = chunk_sum + z_recv[cam].astype(F32)
    y_recv[yh] = chunk_sum.astype(BF16)

    for s in range(1, n_y):
        copy(y_recv.at[yh], y_recv.at[yh], KY, s, dp=(dp + 2 * s) % n_d).start()
    for s in range(1, n_y):
        other = (yh - s + n_y) % n_y
        copy(y_recv.at[other], y_recv.at[other], KY, s, dp=(dp + 2 * s) % n_d).wait_recv()
    all_sum = y_recv[0].astype(F32)
    for s in range(1, n_y):
        all_sum = all_sum + y_recv[s].astype(F32)

    def final_rows(side, index):
        return fin.at[pl.ds(pl.multiple_of(side * lanes + index * chunk, chunk), chunk)]

    fin[pl.ds(pl.multiple_of(core * lanes + z * chunk, chunk), chunk)] = all_sum.astype(BF16)
    for d in range(1, n_z):
        copy(final_rows(core, z), final_rows(core, z), KF, d, view=(z + d) % n_z).start()
    copy(final_rows(core, z), final_rows(core, z), KG, 0, dp=sib).start()
    for d in range(1, n_z):
        cam = (z - d + n_z) % n_z
        copy(final_rows(core, cam), final_rows(core, cam), KF, d, view=cam).wait_recv()
        copy(final_rows(core, cam), final_rows(core, cam), KG, d, dp=sib).start()
    for d in range(n_z):
        cam = (z - d + n_z) % n_z
        copy(final_rows(1 - core, cam), final_rows(1 - core, cam), KG, d, dp=sib).wait_recv()
    g_ref[...] = fin[...].astype(F32)

    for step in range(1, n_t):
        copy(w_ref.at[mine], w_all.at[tm, mine], KW, step, tm=peer(step)).wait_send()
        copy(w_part(step), w_part(step), KS, step, dp=sib).wait_send()
        copy(tok_ref, tok_all.at[tm], KT, step, tm=peer(step)).wait_send()
        copy(cot_ref, cot_all.at[tm], KC, step, tm=peer(step)).wait_send()
        head = (tm + step) % n_t
        copy(xa1.at[head], xb1.at[tm], KB1, step, tm=head).wait_send()
        copy(xa2.at[head], xb2.at[tm], KB2, step, tm=head).wait_send()
    for d in range(1, n_z):
        cam = (z + d) % n_z
        copy(p_send.at[cam], p_all.at[z], KP, d, view=cam).wait_send()
        copy(x1.at[cam], xa1.at[z], KX1, d, view=cam).wait_send()
        copy(x2.at[cam], xa2.at[z], KX2, d, view=cam).wait_send()
        copy(z_send.at[rows_of(cam)], z_recv.at[z], KZ, d, view=cam).wait_send()
        copy(final_rows(core, z), final_rows(core, z), KF, d, view=cam).wait_send()
    core_copy.wait_send()
    for s in range(1, n_y):
        copy(y_recv.at[yh], y_recv.at[yh], KY, s, dp=(dp + 2 * s) % n_d).wait_send()
    for d in range(n_z):
        cam = (z - d + n_z) % n_z
        copy(final_rows(core, cam), final_rows(core, cam), KG, d, dp=sib).wait_send()


def shards(n_d, n_z, n_t, tokens, cotangent, w_query, w_key, w_value, w_out, masks, rig_ids):
    rows, width = tokens.shape[2], tokens.shape[3]
    depth = w_query.shape[1]
    lanes = 2 * depth
    packed = jnp.concatenate([w_query, w_out.T, w_key, w_value], axis=1)
    vmem = pl.BlockSpec(memory_space=pltpu.VMEM)
    smem = pl.BlockSpec(memory_space=pltpu.SMEM)
    half_block = (n_z, rows, lanes)
    most = max(n_z, n_t, n_d)
    attended, grad_rows, grads = pl.pallas_call(
        functools.partial(kernel, n_d, n_z, n_t, depth),
        out_shape=(
            jax.ShapeDtypeStruct((rows, width), BF16),
            jax.ShapeDtypeStruct((rows, width), BF16),
            jax.ShapeDtypeStruct((2 * lanes, width), F32),
        ),
        in_specs=[vmem, vmem, vmem, smem, smem],
        out_specs=(vmem, vmem, vmem),
        scratch_shapes=[
            pltpu.VMEM((n_t, width, 2 * lanes), BF16),
            pltpu.VMEM((n_t, rows, width), BF16),
            pltpu.VMEM((n_t, rows, width), BF16),
            pltpu.VMEM((n_z, rows, 2 * lanes), BF16),
            pltpu.VMEM((n_z, rows, 2 * lanes), BF16),
            pltpu.VMEM((lanes, n_z * rows), BF16),
            pltpu.VMEM((n_z * rows, lanes), F32),
            pltpu.VMEM(half_block, BF16),
            pltpu.VMEM(half_block, BF16),
            pltpu.VMEM(half_block, BF16),
            pltpu.VMEM(half_block, BF16),
            pltpu.VMEM((n_t, rows, lanes), BF16),
            pltpu.VMEM((n_t, rows, lanes), BF16),
            pltpu.VMEM((2 * lanes, width), F32),
            pltpu.VMEM((lanes, width), BF16),
            pltpu.VMEM((lanes, width), BF16),
            pltpu.VMEM((lanes, width), BF16),
            pltpu.VMEM((n_z, lanes // n_z, width), BF16),
            pltpu.VMEM((n_d // 2, lanes // n_z, width), BF16),
            pltpu.VMEM((2 * lanes, width), BF16),
            pltpu.SemaphoreType.DMA((KINDS, most)),
            pltpu.SemaphoreType.DMA((KINDS, most)),
        ],
        compiler_params=pltpu.CompilerParams(
            collective_id=0, has_side_effects=True, vmem_limit_bytes=48 * 1024 * 1024
        ),
        cost_estimate=pl.CostEstimate(
            flops=3_000_000_000, bytes_accessed=8_000_000, transcendentals=1_000_000
        ),
    )(tokens.reshape(rows, width), cotangent.reshape(rows, width), packed, masks, rig_ids)
    return (
        attended.reshape(tokens.shape),
        grad_rows.reshape(tokens.shape),
        grads[:depth].T,
        grads[lanes:lanes + depth].T,
        grads[lanes + depth:].T,
        grads[depth:lanes],
    )


def solution(mesh):
    sizes = mesh.shape
    return jax.shard_map(
        functools.partial(shards, sizes["dp"], sizes["view"], sizes["tm"]),
        mesh=mesh,
        in_specs=(
            P("dp", "view", "tm", None),
            P("dp", "view", "tm", None),
            P(None, "tm"),
            P(None, "tm"),
            P(None, "tm"),
            P("tm", None),
            P(),
            P("dp"),
        ),
        out_specs=(
            P("dp", "view", "tm", None),
            P("dp", "view", "tm", None),
            P(None, "tm"),
            P(None, "tm"),
            P(None, "tm"),
            P("tm", None),
        ),
        check_vma=False,
    )
```

time: 1080 us -> 132 us (0.12)
  waiting for transfers between devices: 979 us -> 0 us
  Pallas kernels: 0 us -> 124 us
  matrix products: 29.7 us -> 0 us
  local copies, waits for them, and re-layouts: 20.7 us -> 6.12 us
  starting transfers between devices: 13.6 us -> 0 us
  between operations: 14.7 us -> 1.37 us
  blocking collectives: 11.9 us -> 0 us
    psum x1 -> x0, waiting for transfers between devices: 553 us -> none  [shards(): lax.psum((query_local, key_local, value_local, out_local), ('dp', 'view'))]
    all_gather x8 -> x0, waiting for transfers between devices: 344 us -> none  [the longest x1 55.6 us: shards(): lax.all_gather(cot_rows, 'tm', axis=0, tiled=True)]
    pallas_call x0 -> x1, Pallas kernels: none -> 124 us  [shards(): pl.pallas_call(functools.partial(kernel, n_d, n_z, n_t, depth), out_shape...]
    unnamed x13 -> x0, waiting for transfers between devices: 77.7 us -> none
    dot_general x17 -> x0, matrix products: 26.1 us -> none  [the longest x1 2.77 us: shards(): jnp.dot(attn_cols.T, cot_all, preferred_element_type=jnp.float32)]
    all_to_all x3 -> x0, starting transfers between devices: 13.2 us -> none  [the longest x1 4.89 us: shards(): lax.all_to_all(grad_value, 'tm', split_axis=1, concat_axis=0, tiled=True)]
    all_to_all x1 -> x0, blocking collectives: 11.9 us -> none  [shards(): lax.all_to_all(grad_query, 'tm', split_axis=1, concat_axis=0, tiled=True)]
    unnamed x36 -> x18, local copies, waits for them, and re-layouts: 16.7 us -> 5.13 us
  transfers between devices with their start and end apart: 14 -> 0, of which waited for: 12 -> 0; matrix products, arithmetic and copies ran while one was open for 4% -> 0% of each run, Pallas kernels for 0% -> 0%
where the time goes in v1:
time: 132 us
  Pallas kernels  124 us (94%)
  local copies, waits for them, and re-layouts  6.12 us (5%)
  between operations  1.37 us (1%)
    pallas_call x1, Pallas kernels, shards(): pl.pallas_call(functools.partial(kernel, n_d, n_z, n_t, depth), out_shape...  124 us
    unnamed x18, local copies, waits for them, and re-layouts  5.13 us

profile of v1, /device:TPU:1, one launch (start us, length us, event | category | flops | bytes accessed | tf_op | source)
XLA Modules:
  0.0 131.8 jit_solution(696629420425546628)
XLA Ops:
  1.3 0.0 copy-start.3
  1.3 1.1 copy.15
  2.4 0.0 copy-done.3
  2.4 0.0 copy-start.4
  2.4 0.2 copy.16
  2.6 0.7 copy-done.4
  3.3 0.0 copy-start.5
  3.3 0.2 copy.17
  3.5 0.7 copy-done.5
  4.2 0.2 copy.14
  4.4 0.0 copy-start
  4.4 0.0 copy-start.1
  4.4 0.0 copy-start.2
  4.4 0.4 pad_maximum_fusion.w_ref
  4.8 0.6 copy-done
  5.4 0.1 copy-done.1
  5.4 0.0 copy-done.2
  5.4 124.0 %shard_map.127 = (bf16[128,1024]{1,0:T(8,128)(2,1)S(1)}, bf16[128,1024]{1,0:T(8,128)(2,1)S(1)}, f32[256,1024]{1,0:T(8,128)S(1)}) custom-call(bf16[128,1024]{1,0:T(8,128)(2,1)S(1)} %bitcast.13, bf16[128,1024]{1,0:T(8,128)(2,1)S(1)} %bitcast.14, bf16[1024,256]{1,0:T(8,128)(2,1)S(1)} %pad_maximum_fusion.w_ref, s32[4,8,8]{2,1,0:T(8,128)S(1)} %copy-done.2, ...), custom_call_target="tpu_custom_call" | custom-call | flops 3000000000 | bytes 8000000 | tf_op jit(solution)/shard_map/pallas_call | solution.py:331
  129.5 1.0 fusion
  130.4 0.7 copy.21
  131.1 0.7 copy.22
Async XLA Ops:
  1.3 1.1 copy-start.3
  2.4 0.9 copy-start.4
  3.3 0.9 copy-start.5
  4.4 1.0 copy-start
  4.4 1.0 copy-start.1
  4.4 1.0 copy-start.2

commit v2 on v1

--- a/solution.py
+++ b/solution.py
@@ -11,8 +11,8 @@
 BF16 = jnp.bfloat16
 F32 = jnp.float32
 
-KW, KS, KT, KC, KP, KX1, KX2, KB1, KB2, KR, KZ, KY, KF, KG = range(14)
-KINDS = 14
+(KW, KV1, KV2, KS1, KS2, KT1, KT2, KC1, KC2, KP, KX1, KX2, KB1, KB2, KR, KZ, KY, KF, KG) = range(19)
+KINDS = 19
 
 NT = (((1,), (1,)), ((), ()))
 
@@ -27,13 +27,13 @@
 
 def kernel(
     n_d, n_z, n_t, depth,
-    tok_ref, cot_ref, w_ref, masks_ref, rig_ref,
+    tok_hbm, cot_hbm, wq_hbm, wk_hbm, wv_hbm, wo_hbm, masks_ref, rig_ref,
     att_ref, gtok_ref, g_ref,
-    w_all, tok_all, cot_all, p_send, p_all, kv_t, acc, x1, x2, xa1, xa2, xb1, xb2,
+    w_in, wo_in, w_all, tok_all, cot_all, p_send, p_all, kv_t, acc, x1, x2, xa1, xa2, xb1, xb2,
     g_sum, c_send, c_recv, z_send, z_recv, y_recv, fin,
-    ssem, rsem,
+    lsem, ssem, rsem,
 ):
-    rows, width = tok_ref.shape
+    rows, width = tok_hbm.shape
     lanes = 2 * depth
     n_x = n_t // 2
     n_y = n_d // 2
@@ -41,6 +41,18 @@
     core, yh = dp % 2, dp // 2
     x, yl = tm // 2, tm % 2
     sib = dp + 1 - 2 * core
+    pair = x * 2 + 1 - yl
+    beyond = ((yh - 1 + 2 * yl + n_y) % n_y) * 2 + core
+
+    loads = [
+        pltpu.make_async_copy(src, dst, lsem.at[at])
+        for at, (src, dst) in enumerate([
+            (wq_hbm, w_in.at[0]), (wk_hbm, w_in.at[1]), (wv_hbm, w_in.at[2]), (wo_hbm, wo_in),
+            (tok_hbm, tok_all.at[tm]), (cot_hbm, cot_all.at[tm]),
+        ])
+    ]
+    for load in loads:
+        load.start()
 
     def copy(src, dst, kind, at, **to):
         return pltpu.make_async_remote_copy(
@@ -49,49 +61,63 @@
         )
 
     barrier = pltpu.get_barrier_semaphore()
-    greeted = 0
-    for s in range(1, n_t):
-        pl.semaphore_signal(barrier, inc=1, device_id={"tm": (tm + s) % n_t}, device_id_type=MESH)
-        greeted += 1
-    for s in range(1, n_z):
-        pl.semaphore_signal(barrier, inc=1, device_id={"view": (z + s) % n_z}, device_id_type=MESH)
-        greeted += 1
-    for s in range(1, n_y):
-        pl.semaphore_signal(barrier, inc=1, device_id={"dp": (dp + 2 * s) % n_d}, device_id_type=MESH)
-        greeted += 1
-    pl.semaphore_signal(barrier, inc=1, device_id={"dp": sib}, device_id_type=MESH)
-    greeted += 1
-    pl.semaphore_wait(barrier, greeted)
-
-    def offsets(step):
-        g = step // 2
-        dx = g + g // 2 - 2 * (g // 3) if n_x == 4 else g
-        return dx, step % 2
-
-    def peer(step):
-        dx, dy = offsets(step)
-        return ((x + dx) % n_x) * 2 + (yl + dy) % 2
-
-    def source(step):
-        dx, dy = offsets(step)
-        return ((x - dx + n_x) % n_x) * 2 + (yl + dy) % 2
-
-    half = width // 2
-    mine = pl.ds(pl.multiple_of(core * half, half), half)
-    for step in range(1, n_t):
-        copy(w_ref.at[mine], w_all.at[tm, mine], KW, step, tm=peer(step)).start()
-    w_all[tm] = w_ref[...]
-    tok_all[tm] = tok_ref[...]
-    cot_all[tm] = cot_ref[...]
+    friends = [{"tm": (tm + s) % n_t} for s in range(1, n_t)]
+    friends += [{"view": (z + s) % n_z} for s in range(1, n_z)]
+    friends += [{"dp": (dp + 2 * s) % n_d} for s in range(1, n_y)]
+    friends += [{"dp": sib}, {"dp": beyond, "tm": pair}]
+    for friend in friends:
+        pl.semaphore_signal(barrier, inc=1, device_id=friend, device_id_type=MESH)
+    for load in loads[:4]:
+        load.wait()
+    w_all[tm, :, :lanes] = jnp.concatenate([w_in[0], wo_in[...].T], axis=1)
+    w_all[tm, :, lanes:] = jnp.concatenate([w_in[1], w_in[2]], axis=1)
+    pl.semaphore_wait(barrier, len(friends))
+
+    def ahead(dx, side):
+        return ((x + dx) % n_x) * 2 + side
+
+    def behind(dx, side):
+        return ((x - dx + n_x) % n_x) * 2 + side
+
+    half, quarter = width // 2, width // 4
+
+    def w_rows(head, start, size):
+        return w_all.at[head, pl.ds(pl.multiple_of(start, size), size)]
+
+    def w_mine(head):
+        return w_rows(head, core * half, half)
+
+    def w_along(dx):
+        return copy(w_mine(tm), w_mine(tm), KW, dx, tm=ahead(dx, yl))
+
+    def w_across(dx):
+        head = behind(dx, yl)
+        near = w_rows(head, core * half, quarter)
+        far = w_rows(head, core * half + quarter, quarter)
+        return copy(near, near, KV1, dx, tm=pair), copy(far, far, KV2, dx, dp=beyond, tm=pair)
+
+    def w_share(dx, side, kind):
+        part = w_mine(behind(dx, side))
+        return copy(part, part, kind, dx, dp=sib)
+
+    def w_shared(dx, side, kind):
+        part = w_rows(behind(dx, side), (1 - core) * half, half)
+        return copy(part, part, kind, dx, dp=sib)
+
+    x_order = [1, 3, 2] if n_x == 4 else list(range(1, n_x))
+    for dx in x_order:
+        w_along(dx).start()
+    for part in w_across(0):
+        part.start()
+    for load in loads[4:]:
+        load.wait()
 
     first = lax.broadcasted_iota(jnp.int32, (rows, lanes), 1) < depth
 
     def project(head):
-        weights = w_all[head]
-        by_tok = dot(tok_ref[...], weights)
-        by_cot = dot(cot_ref[...], weights[:, :lanes])
-        p_send[head, :, :lanes] = jnp.where(first, by_tok[:, :lanes], by_cot).astype(BF16)
-        p_send[head, :, lanes:] = by_tok[:, lanes:].astype(BF16)
+        both = dot(jnp.concatenate([tok_all[tm], cot_all[tm]], axis=0), w_all[head])
+        p_send[head, :, :lanes] = jnp.where(first, both[:rows, :lanes], both[rows:, :lanes]).astype(BF16)
+        p_send[head, :, lanes:] = both[:rows, lanes:].astype(BF16)
 
         @pl.when(head == z)
         def _():
@@ -101,36 +127,72 @@
         def _():
             copy(p_send.at[head], p_all.at[z], KP, (head - z + n_z) % n_z, view=head).start()
 
-    def w_part(step):
-        return w_all.at[source(step), mine]
-
-    def w_step(step, _):
-        copy(w_part(step), w_part(step), KW, step, tm=peer(step)).wait_recv()
-        copy(w_part(step), w_part(step), KS, step, dp=sib).start()
-
-        @pl.when(step > 1)
-        def _():
-            w_other(step - 1)
-
-        project(source(step - 1))
+    project(tm)
+    for dx in x_order:
+        copy(w_mine(behind(dx, yl)), w_mine(behind(dx, yl)), KW, dx, tm=ahead(dx, yl)).wait_recv()
+        for part in w_across(dx):
+            part.start()
+        w_share(dx, yl, KS1).start()
+
+    def cot_along(dx):
+        return copy(cot_all.at[tm], cot_all.at[tm], KC1, dx, tm=ahead(dx, yl))
+
+    for dx in x_order:
+        cot_along(dx).start()
+
+    def x_heads(i, _):
+        dx = 1 + (i + z) % (n_x - 1)
+        w_shared(dx, yl, KS1).wait_recv()
+        project(behind(dx, yl))
         return 0
 
-    theirs = pl.ds(pl.multiple_of((1 - core) * half, half), half)
-
-    def w_other(step):
-        part = w_all.at[source(step), theirs]
-        copy(part, part, KS, step, dp=sib).wait_recv()
-
-    lax.fori_loop(1, n_t, w_step, 0)
-    w_other(n_t - 1)
-    project(source(n_t - 1))
-
-    for step in range(1, n_t):
-        copy(tok_ref, tok_all.at[tm], KT, step, tm=peer(step)).start()
-        copy(cot_ref, cot_all.at[tm], KC, step, tm=peer(step)).start()
+    if n_x > 1:
+        lax.fori_loop(0, n_x - 1, x_heads, 0)
+    for dx in [0] + x_order:
+        head = behind(dx, 1 - yl)
+        near = w_rows(head, core * half, quarter)
+        far = w_rows(head, core * half + quarter, quarter)
+        copy(near, near, KV1, dx, tm=pair).wait_recv()
+        copy(far, far, KV2, dx, dp=beyond, tm=pair).wait_recv()
+        w_share(dx, 1 - yl, KS2).start()
+
+    def tok_pair():
+        return copy(tok_all.at[tm], tok_all.at[tm], KT1, 0, tm=pair)
+
+    def tok_along(dx, span, kind):
+        return copy(tok_all.at[span], tok_all.at[span], kind, dx, tm=ahead(dx, yl))
+
+    def cot_pair(dx):
+        span = behind(dx, yl)
+        return copy(cot_all.at[span], cot_all.at[span], KC2, dx, tm=pair)
+
+    tok_pair().start()
+    cot_pair(0).start()
+    for dx in x_order:
+        tok_along(dx, tm, KT1).start()
+
+    def y_heads(i, _):
+        dx = (i + z) % n_x
+        w_shared(dx, 1 - yl, KS2).wait_recv()
+        project(behind(dx, 1 - yl))
+        return 0
+
+    lax.fori_loop(0, n_x, y_heads, 0)
+
+    def tok_forward():
+        copy(tok_all.at[pair], tok_all.at[pair], KT1, 0, tm=pair).wait_recv()
+        for dx in x_order:
+            tok_along(dx, pair, KT2).start()
+
+    def cot_forward():
+        for dx in x_order:
+            span = behind(dx, yl)
+            copy(cot_all.at[span], cot_all.at[span], KC1, dx, tm=ahead(dx, yl)).wait_recv()
+            cot_pair(dx).start()
 
     for d in range(1, n_z):
         copy(p_send.at[0], p_all.at[(z - d + n_z) % n_z], KP, d, view=(z + d) % n_z).wait_recv()
+    tok_forward()
 
     total = n_z * rows
     kv_t[...] = p_all[:, :, lanes:].reshape(total, lanes).T
@@ -138,7 +200,13 @@
     rig = rig_ref[0]
     factor = depth ** -0.5
 
-    def attend(cam, _):
+    def attend(step, _):
+        cam = (z + 1 + step) % n_z
+
+        @pl.when(step == n_z // 2)
+        def _():
+            cot_forward()
+
         qd = p_all[cam, :, :lanes]
         zero = jnp.zeros_like(qd)
         block = jnp.concatenate([jnp.where(first, qd, zero), jnp.where(first, zero, qd)], axis=0)
@@ -210,17 +278,20 @@
         hand_on(xa2, xb2, KB2, head)
         return 0
 
-    lax.fori_loop(0, n_z, arrive1, 0)
-    lax.fori_loop(0, n_z, arrive2, 0)
+    lax.fori_loop(0, n_z, lambda i, _: arrive1((i + tm) % n_z, _), 0)
+    lax.fori_loop(0, n_z, lambda i, _: arrive2((i + tm) % n_z, _), 0)
 
     for f in range(1, n_t):
         span = (tm - f + n_t) % n_t
         copy(xb1.at[span], xb1.at[span], KB1, f, tm=span).wait_recv()
         copy(xb2.at[span], xb2.at[span], KB2, f, tm=span).wait_recv()
-    for step in range(1, n_t):
-        span = source(step)
-        copy(tok_all.at[span], tok_all.at[span], KT, step, tm=peer(step)).wait_recv()
-        copy(cot_all.at[span], cot_all.at[span], KC, step, tm=peer(step)).wait_recv()
+    for dx in x_order:
+        span, other = behind(dx, yl), behind(dx, 1 - yl)
+        copy(tok_all.at[span], tok_all.at[span], KT1, dx, tm=ahead(dx, yl)).wait_recv()
+        copy(tok_all.at[other], tok_all.at[other], KT2, dx, tm=ahead(dx, yl)).wait_recv()
+    for dx in [0] + x_order:
+        other = behind(dx, 1 - yl)
+        copy(cot_all.at[other], cot_all.at[other], KC2, dx, tm=pair).wait_recv()
 
     b1 = xb1[...].reshape(n_t * rows, lanes).T
     b2 = xb2[...].reshape(n_t * rows, lanes).T
@@ -296,11 +367,16 @@
         copy(final_rows(1 - core, cam), final_rows(1 - core, cam), KG, d, dp=sib).wait_recv()
     g_ref[...] = fin[...].astype(F32)
 
+    for dx in [0] + x_order:
+        gone = [*w_across(dx), w_share(dx, 1 - yl, KS2), cot_pair(dx)]
+        if dx:
+            gone += [w_along(dx), w_share(dx, yl, KS1), cot_along(dx)]
+            gone += [tok_along(dx, tm, KT1), tok_along(dx, pair, KT2)]
+        else:
+            gone += [tok_pair()]
+        for one in gone:
+            one.wait_send()
     for step in range(1, n_t):
-        copy(w_ref.at[mine], w_all.at[tm, mine], KW, step, tm=peer(step)).wait_send()
-        copy(w_part(step), w_part(step), KS, step, dp=sib).wait_send()
-        copy(tok_ref, tok_all.at[tm], KT, step, tm=peer(step)).wait_send()
-        copy(cot_ref, cot_all.at[tm], KC, step, tm=peer(step)).wait_send()
         head = (tm + step) % n_t
         copy(xa1.at[head], xb1.at[tm], KB1, step, tm=head).wait_send()
         copy(xa2.at[head], xb2.at[tm], KB2, step, tm=head).wait_send()
@@ -323,9 +399,9 @@
     rows, width = tokens.shape[2], tokens.shape[3]
     depth = w_query.shape[1]
     lanes = 2 * depth
-    packed = jnp.concatenate([w_query, w_out.T, w_key, w_value], axis=1)
     vmem = pl.BlockSpec(memory_space=pltpu.VMEM)
     smem = pl.BlockSpec(memory_space=pltpu.SMEM)
+    hbm = pl.BlockSpec(memory_space=pl.ANY)
     half_block = (n_z, rows, lanes)
     most = max(n_z, n_t, n_d)
     attended, grad_rows, grads = pl.pallas_call(
@@ -335,9 +411,11 @@
             jax.ShapeDtypeStruct((rows, width), BF16),
             jax.ShapeDtypeStruct((2 * lanes, width), F32),
         ),
-        in_specs=[vmem, vmem, vmem, smem, smem],
+        in_specs=[hbm] * 6 + [smem] * 2,
         out_specs=(vmem, vmem, vmem),
         scratch_shapes=[
+            pltpu.VMEM((3, width, depth), BF16),
+            pltpu.VMEM((depth, width), BF16),
             pltpu.VMEM((n_t, width, 2 * lanes), BF16),
             pltpu.VMEM((n_t, rows, width), BF16),
             pltpu.VMEM((n_t, rows, width), BF16),
@@ -358,6 +436,7 @@
             pltpu.VMEM((n_z, lanes // n_z, width), BF16),
             pltpu.VMEM((n_d // 2, lanes // n_z, width), BF16),
             pltpu.VMEM((2 * lanes, width), BF16),
+            pltpu.SemaphoreType.DMA((6,)),
             pltpu.SemaphoreType.DMA((KINDS, most)),
             pltpu.SemaphoreType.DMA((KINDS, most)),
         ],
@@ -367,7 +446,8 @@
         cost_estimate=pl.CostEstimate(
             flops=3_000_000_000, bytes_accessed=8_000_000, transcendentals=1_000_000
         ),
-    )(tokens.reshape(rows, width), cotangent.reshape(rows, width), packed, masks, rig_ids)
+    )(tokens.reshape(rows, width), cotangent.reshape(rows, width), w_query, w_key, w_value, w_out,
+      masks, rig_ids)
     return (
         attended.reshape(tokens.shape),
         grad_rows.reshape(tokens.shape),

time: 132 us -> 111 us (0.84)
  Pallas kernels: 124 us -> 105 us
  local copies, waits for them, and re-layouts: 6.12 us -> 4.67 us
    pallas_call x1, Pallas kernels: 124 us -> 105 us  [shards(): pl.pallas_call(functools.partial(kernel, n_d, n_z, n_t, depth), out_shape...]
    unnamed x18 -> x17, local copies, waits for them, and re-layouts: 5.13 us -> 3.69 us
where the time goes in v2:
time: 111 us
  Pallas kernels  105 us (95%)
  local copies, waits for them, and re-layouts  4.67 us (4%)
  between operations  1.37 us (1%)
    pallas_call x1, Pallas kernels, shards(): pl.pallas_call(functools.partial(kernel, n_d, n_z, n_t, depth), out_shape...  105 us
    unnamed x17, local copies, waits for them, and re-layouts  3.69 us

profile of v2, /device:TPU:1, one launch (start us, length us, event | category | flops | bytes accessed | tf_op | source)
XLA Modules:
  0.0 110.7 jit_solution(14775230202800057944)
XLA Ops:
  1.3 0.0 copy-start.4
  1.3 0.0 copy-start.5
  1.3 1.1 %copy.14.wq_hbm = bf16[1024,64]{1,0:T(8,128)(2,1)S(1)} copy(bf16[1024,64]{0,1:T(8,128)(2,1)} %param.10) | data formatting | bytes 262144 | tf_op args[2]
  2.4 0.0 copy-done.4
  2.4 0.0 copy-start.1
  2.4 0.0 copy-start.3
  2.5 0.2 copy.15.wk_hbm
  2.6 0.0 copy-done.5
  2.6 0.0 copy-start
  2.7 0.0 copy-start.2
  2.7 0.2 copy.16.wv_hbm
  2.8 0.5 copy-done.1
  3.4 0.0 copy-done.3
  3.4 0.2 copy-done
  3.6 0.0 copy-done.2
  3.6 104.7 %shard_map.127 = (bf16[128,1024]{1,0:T(8,128)(2,1)S(1)}, bf16[128,1024]{1,0:T(8,128)(2,1)S(1)}, f32[256,1024]{1,0:T(8,128)S(1)}) custom-call(bf16[128,1024]{1,0:T(8,128)(2,1)S(1)} %bitcast.12, bf16[128,1024]{1,0:T(8,128)(2,1)S(1)} %bitcast.13, bf16[1024,64]{1,0:T(8,128)(2,1)S(1)} %copy.14.wq_hbm, bf16[1024,64]{1,0:T(8,128)(2,1)S(1)} %copy.15.wk_hbm, ...), custom_call_target="tpu_custom_call" | custom-call | flops 3000000000 | bytes 8000000 | tf_op jit(solution)/shard_map/pallas_call | solution.py:407
  108.3 1.0 fusion
  109.3 0.7 copy.20
  110.0 0.7 copy.21
Async XLA Ops:
  1.3 1.1 %copy-start.4 = (bf16[1024,64]{0,1:T(8,128)(2,1)S(1)}, bf16[1024,64]{0,1:T(8,128)(2,1)}, u32[]{:S(2)}) copy-start(bf16[1024,64]{0,1:T(8,128)(2,1)} %param.11) | copy-start | bytes 393220
  1.3 1.3 %copy-start.5 = (bf16[1024,64]{0,1:T(8,128)(2,1)S(1)}, bf16[1024,64]{0,1:T(8,128)(2,1)}, u32[]{:S(2)}) copy-start(bf16[1024,64]{0,1:T(8,128)(2,1)} %param.12) | copy-start | bytes 393220
  2.4 1.0 copy-start.1
  2.4 0.9 copy-start.3
  2.6 1.0 copy-start
  2.7 1.0 copy-start.2

commit v3 on v2

v3 whole, which is shorter than its diff:
```python
import functools

import jax
import jax.numpy as jnp
from jax import lax
from jax.experimental import pallas as pl
from jax.experimental.pallas import tpu as pltpu
from jax.sharding import PartitionSpec as P

MESH = pl.DeviceIdType.MESH
BF16 = jnp.bfloat16
F32 = jnp.float32

(KW, KV1, KV2, KS1, KS2, KT1, KT2, KC1, KC2, KP, KX1, KX2, KB1, KB2, KR, KZ, KY, KF, KG) = range(19)
KINDS = 19

NT = (((1,), (1,)), ((), ()))


def dot(a, b):
    return jnp.dot(a, b, preferred_element_type=F32)


def dot_nt(a, b):
    return lax.dot_general(a, b, NT, preferred_element_type=F32)


def kernel(
    n_d, n_z, n_t, depth,
    tok_hbm, cot_hbm, wq_hbm, wk_hbm, wv_hbm, wo_hbm, masks_ref, rig_ref,
    att_ref, gtok_ref, g_ref,
    w_all, tok_all, cot_all, p_send, p_all, kv_t, pairs, x1, x2, xa1, xa2, xb1, xb2,
    g_sum, c_send, c_recv, z_send, z_recv, y_recv, fin,
    lsem, ssem, rsem,
):
    rows, width = tok_hbm.shape
    lanes = 2 * depth
    n_x = n_t // 2
    n_y = n_d // 2
    dp, z, tm = lax.axis_index("dp"), lax.axis_index("view"), lax.axis_index("tm")
    core, yh = dp % 2, dp // 2
    x, yl = tm // 2, tm % 2
    sib = dp + 1 - 2 * core
    pair = x * 2 + 1 - yl
    beyond = ((yh - 1 + 2 * yl + n_y) % n_y) * 2 + core

    loads = [
        pltpu.make_async_copy(src, dst, lsem.at[at])
        for at, (src, dst) in enumerate([
            (wq_hbm, w_all.at[tm, pl.ds(0, depth)]), (wo_hbm, w_all.at[tm, pl.ds(depth, depth)]),
            (wk_hbm, w_all.at[tm, pl.ds(lanes, depth)]),
            (wv_hbm, w_all.at[tm, pl.ds(lanes + depth, depth)]),
            (tok_hbm, tok_all.at[tm]), (cot_hbm, cot_all.at[tm]),
        ])
    ]
    for load in loads:
        load.start()

    def copy(src, dst, kind, at, **to):
        return pltpu.make_async_remote_copy(
            src_ref=src, dst_ref=dst, send_sem=ssem.at[kind, at], recv_sem=rsem.at[kind, at],
            device_id=to, device_id_type=MESH,
        )

    barrier = pltpu.get_barrier_semaphore()
    friends = [{"tm": (tm + s) % n_t} for s in range(1, n_t)]
    friends += [{"view": (z + s) % n_z} for s in range(1, n_z)]
    friends += [{"dp": (dp + 2 * s) % n_d} for s in range(1, n_y)]
    friends += [{"dp": sib}, {"dp": beyond, "tm": pair}]
    for friend in friends:
        pl.semaphore_signal(barrier, inc=1, device_id=friend, device_id_type=MESH)
    for load in loads:
        load.wait()
    pl.semaphore_wait(barrier, len(friends))

    def ahead(dx, side):
        return ((x + dx) % n_x) * 2 + side

    def behind(dx, side):
        return ((x - dx + n_x) % n_x) * 2 + side

    half, quarter = lanes, depth

    def w_rows(head, start, size):
        return w_all.at[head, pl.ds(pl.multiple_of(start, size), size)]

    def w_mine(head):
        return w_rows(head, core * half, half)

    def w_along(dx):
        return copy(w_mine(tm), w_mine(tm), KW, dx, tm=ahead(dx, yl))

    def w_across(dx):
        head = behind(dx, yl)
        near = w_rows(head, core * half, quarter)
        far = w_rows(head, core * half + quarter, quarter)
        return copy(near, near, KV1, dx, tm=pair), copy(far, far, KV2, dx, dp=beyond, tm=pair)

    def w_share(dx, side, kind):
        part = w_mine(behind(dx, side))
        return copy(part, part, kind, dx, dp=sib)

    def w_shared(dx, side, kind):
        part = w_rows(behind(dx, side), (1 - core) * half, half)
        return copy(part, part, kind, dx, dp=sib)

    x_order = [1, 3, 2] if n_x == 4 else list(range(1, n_x))
    for dx in x_order:
        w_along(dx).start()
    for part in w_across(0):
        part.start()

    def tok_pair():
        return copy(tok_all.at[tm], tok_all.at[tm], KT1, 0, tm=pair)

    def tok_along(dx, span, kind):
        return copy(tok_all.at[span], tok_all.at[span], kind, dx, tm=ahead(dx, yl))

    def cot_pair(dx):
        span = behind(dx, yl)
        return copy(cot_all.at[span], cot_all.at[span], KC2, dx, tm=pair)

    def cot_along(dx):
        return copy(cot_all.at[tm], cot_all.at[tm], KC1, dx, tm=ahead(dx, yl))

    tok_pair().start()

    first = lax.broadcasted_iota(jnp.int32, (rows, lanes), 1) < depth

    def project(head):
        both = dot_nt(jnp.concatenate([tok_all[tm], cot_all[tm]], axis=0), w_all[head])
        p_send[head, :, :lanes] = jnp.where(first, both[:rows, :lanes], both[rows:, :lanes]).astype(BF16)
        p_send[head, :, lanes:] = both[:rows, lanes:].astype(BF16)

        @pl.when(head == z)
        def _():
            p_all[z] = p_send[head]

        @pl.when(head != z)
        def _():
            copy(p_send.at[head], p_all.at[z], KP, (head - z + n_z) % n_z, view=head).start()

    project(tm)
    for dx in x_order:
        copy(w_mine(behind(dx, yl)), w_mine(behind(dx, yl)), KW, dx, tm=ahead(dx, yl)).wait_recv()
        for part in w_across(dx):
            part.start()
        w_share(dx, yl, KS1).start()

    for dx in x_order:
        cot_along(dx).start()

    def x_heads(i, _):
        dx = 1 + (i + z) % (n_x - 1)
        w_shared(dx, yl, KS1).wait_recv()
        project(behind(dx, yl))
        return 0

    if n_x > 1:
        lax.fori_loop(0, n_x - 1, x_heads, 0)
    for dx in [0] + x_order:
        head = behind(dx, 1 - yl)
        near = w_rows(head, core * half, quarter)
        far = w_rows(head, core * half + quarter, quarter)
        copy(near, near, KV1, dx, tm=pair).wait_recv()
        copy(far, far, KV2, dx, dp=beyond, tm=pair).wait_recv()
        w_share(dx, 1 - yl, KS2).start()

    cot_pair(0).start()
    for dx in x_order:
        tok_along(dx, tm, KT1).start()

    def y_heads(i, _):
        dx = (i + z) % n_x
        w_shared(dx, 1 - yl, KS2).wait_recv()
        project(behind(dx, 1 - yl))
        return 0

    lax.fori_loop(0, n_x, y_heads, 0)

    def tok_forward():
        copy(tok_all.at[pair], tok_all.at[pair], KT1, 0, tm=pair).wait_recv()
        for dx in x_order:
            tok_along(dx, pair, KT2).start()

    def cot_forward():
        for dx in x_order:
            span = behind(dx, yl)
            copy(cot_all.at[span], cot_all.at[span], KC1, dx, tm=ahead(dx, yl)).wait_recv()
            cot_pair(dx).start()

    for d in range(1, n_z):
        copy(p_send.at[0], p_all.at[(z - d + n_z) % n_z], KP, d, view=(z + d) % n_z).wait_recv()
    tok_forward()

    total = n_z * rows
    kv_t[...] = p_all[:, :, lanes:].reshape(total, lanes).T
    rig = rig_ref[0]
    factor = depth ** -0.5

    def split(cam):
        qd = p_all[cam, :, :lanes]
        zero = jnp.zeros_like(qd)
        return jnp.where(first, qd, zero), jnp.where(first, zero, qd)

    def attend(step, _):
        cams = [(z + 1 + 2 * step) % n_z, (z + 2 + 2 * step) % n_z]

        @pl.when(step == 1)
        def _():
            cot_forward()

        query0, grad0 = split(cams[0])
        query1, grad1 = split(cams[1])
        kv = p_all[:, :, lanes:].reshape(total, lanes)
        both = dot_nt(kv, jnp.concatenate([query0, query1, grad0, grad1], axis=0))
        scores = jnp.concatenate(
            [
                jnp.concatenate(
                    [
                        both[b * rows:(b + 1) * rows, q * rows:(q + 1) * rows] * factor
                        + (masks_ref[rig, cams[q], b] - 1).astype(F32) * 1e30
                        for q in range(2)
                    ],
                    axis=1,
                )
                for b in range(n_z)
            ],
            axis=0,
        )
        weights = jnp.exp(scores - jnp.max(scores, axis=0, keepdims=True))
        probs = weights * (1.0 / jnp.sum(weights, axis=0, keepdims=True))
        probs_half = probs.astype(BF16)
        attn = dot(kv_t[depth:], probs_half)
        grad_attn = jnp.concatenate(
            [(query0 + grad0).astype(F32).T[depth:], (query1 + grad1).astype(F32).T[depth:]], axis=1
        )
        delta = jnp.sum(grad_attn * attn.astype(BF16).astype(F32), axis=0, keepdims=True)
        dscore = (probs * (both[:, 2 * rows:] - delta) * factor).astype(BF16)
        dq = dot(kv_t[:depth], dscore)
        out = jnp.concatenate([dq, attn], axis=0)
        for q, cam in enumerate(cams):
            cols = slice(q * rows, (q + 1) * rows)
            x1[cam] = out[:, cols].T.astype(BF16)

            @pl.when(cam == z)
            def _():
                xa1[z] = x1[cam]

            @pl.when(cam != z)
            def _():
                copy(x1.at[cam], xa1.at[z], KX1, (cam - z + n_z) % n_z, view=cam).start()

            pairs[cam, :, :rows] = dscore[:, cols]
            pairs[cam, :, rows:] = probs_half[:, cols]
        return 0

    lax.fori_loop(0, n_z // 2, attend, 0)

    def keys(step, _):
        cams = [(z + 1 + 2 * step) % n_z, (z + 2 + 2 * step) % n_z]
        sums = jnp.zeros((2 * rows, lanes), F32)
        for query in range(n_z):
            block = jnp.concatenate(split(query), axis=0)
            left = jnp.concatenate(
                [pairs[query, pl.ds(pl.multiple_of(cam * rows, rows), rows)] for cam in cams], axis=0
            )
            sums = sums + dot(left, block).astype(BF16).astype(F32)
        for k, cam in enumerate(cams):
            x2[cam] = sums[k * rows:(k + 1) * rows].astype(BF16)

            @pl.when(cam == z)
            def _():
                xa2[z] = x2[cam]

            @pl.when(cam != z)
            def _():
                copy(x2.at[cam], xa2.at[z], KX2, (cam - z + n_z) % n_z, view=cam).start()
        return 0

    lax.fori_loop(0, n_z // 2, keys, 0)

    def hand_on(src, dst, kind, head):
        @pl.when(head == tm)
        def _():
            dst[tm] = src[head]

        @pl.when(head != tm)
        def _():
            copy(src.at[head], dst.at[tm], kind, (head - tm + n_t) % n_t, tm=head).start()

    def arrive1(d, _):
        head = (z - d + n_z) % n_z

        @pl.when(d > 0)
        def _():
            copy(xa1.at[head], xa1.at[head], KX1, d, view=head).wait_recv()

        hand_on(xa1, xb1, KB1, head)
        return 0

    def arrive2(d, _):
        head = (z - d + n_z) % n_z

        @pl.when(d > 0)
        def _():
            copy(xa2.at[head], xa2.at[head], KX2, d, view=head).wait_recv()

        hand_on(xa2, xb2, KB2, head)
        return 0

    lax.fori_loop(0, n_z, lambda i, _: arrive1((i + tm) % n_z, _), 0)
    lax.fori_loop(0, n_z, lambda i, _: arrive2((i + tm) % n_z, _), 0)

    def handed(ref, kind):
        for f in range(1, n_t):
            span = (tm - f + n_t) % n_t
            copy(ref.at[span], ref.at[span], kind, f, tm=span).wait_recv()

    chunk = width // n_z
    keep = pl.multiple_of(core * depth, depth)
    give = pl.multiple_of((1 - core) * depth, depth)

    def core_copy(p):
        return copy(c_send.at[p], c_recv.at[p], KR, p, dp=sib)

    def camera_copy(p, d):
        cam = (z + d) % n_z
        return copy(z_send.at[p, cam], z_recv.at[p, z], KZ, p * n_z + d, view=cam)

    def clip_copy(p, s):
        part = y_recv.at[p, yh]
        return copy(part, part, KY, p * n_y + s, dp=(dp + 2 * s) % n_d)

    def final_copy(p, d):
        part = fin.at[p, core, z]
        return copy(part, part, KF, p * n_z + d, view=(z + d) % n_z)

    def final_share(p, d):
        part = fin.at[p, core, (z - d + n_z) % n_z]
        return copy(part, part, KG, p * n_z + d, dp=sib)

    def core_start(p):
        c_send[p] = g_sum[p, pl.ds(give, depth)].astype(BF16)
        core_copy(p).start()

    def camera_start(p):
        core_copy(p).wait_recv()
        total = (g_sum[p, pl.ds(keep, depth)] + c_recv[p].astype(F32)).astype(BF16)
        for cam in range(n_z):
            z_send[p, cam] = total[:, cam * chunk:(cam + 1) * chunk]
        for d in range(1, n_z):
            camera_copy(p, d).start()

    def clip_start(p):
        total = z_send[p, z].astype(F32)
        for d in range(1, n_z):
            cam = (z - d + n_z) % n_z
            copy(z_recv.at[p, cam], z_recv.at[p, cam], KZ, p * n_z + d, view=cam).wait_recv()
            total = total + z_recv[p, cam].astype(F32)
        y_recv[p, yh] = total.astype(BF16)
        for s in range(1, n_y):
            clip_copy(p, s).start()

    def spread_start(p):
        for s in range(1, n_y):
            other = y_recv.at[p, (yh - s + n_y) % n_y]
            copy(other, other, KY, p * n_y + s, dp=(dp + 2 * s) % n_d).wait_recv()
        total = y_recv[p, 0].astype(F32)
        for s in range(1, n_y):
            total = total + y_recv[p, s].astype(F32)
        fin[p, core, z] = total.astype(BF16)
        for d in range(1, n_z):
            final_copy(p, d).start()
        final_share(p, 0).start()

    def spread_forward(p):
        for d in range(1, n_z):
            part = fin.at[p, core, (z - d + n_z) % n_z]
            copy(part, part, KF, p * n_z + d, view=(z + d) % n_z).wait_recv()
            final_share(p, d).start()

    def spread_end(p):
        for d in range(n_z):
            part = fin.at[p, 1 - core, (z - d + n_z) % n_z]
            copy(part, part, KG, p * n_z + d, dp=sib).wait_recv()
        for side in range(2):
            for cam in range(n_z):
                place = (slice((2 * p + side) * depth, (2 * p + side + 1) * depth),
                         slice(cam * chunk, (cam + 1) * chunk))
                g_ref[place] = fin[p, side, cam].astype(F32)

    def finish(head, sums):
        one, two = xa1[head], xa2[head]
        zero = jnp.zeros_like(one)
        left = jnp.concatenate(
            [
                jnp.concatenate([jnp.where(first, one, zero), two], axis=1),
                jnp.concatenate([jnp.where(first, zero, one), zero], axis=1),
            ],
            axis=0,
        )
        return sums + dot(left, w_all[head])

    for dx in x_order:
        span, other = behind(dx, yl), behind(dx, 1 - yl)
        copy(tok_all.at[span], tok_all.at[span], KT1, dx, tm=ahead(dx, yl)).wait_recv()
        copy(tok_all.at[other], tok_all.at[other], KT2, dx, tm=ahead(dx, yl)).wait_recv()
    for dx in [0] + x_order:
        other = behind(dx, 1 - yl)
        copy(cot_all.at[other], cot_all.at[other], KC2, dx, tm=pair).wait_recv()
    tokens = tok_all[...].reshape(n_t * rows, width)
    cots = cot_all[...].reshape(n_t * rows, width)
    handed(xb1, KB1)
    b1 = xb1[...].reshape(n_t * rows, lanes).T
    g_sum[0, :depth] = dot(b1[:depth], tokens)
    g_sum[0, depth:] = dot(b1[depth:], cots)
    core_start(0)
    handed(xb2, KB2)
    g_sum[1] = dot(xb2[...].reshape(n_t * rows, lanes).T, tokens)
    camera_start(0)
    core_start(1)
    camera_start(1)
    sums = lax.fori_loop(0, n_z // 2, finish, jnp.zeros((2 * rows, width), F32))
    clip_start(0)
    sums = lax.fori_loop(n_z // 2, n_z, finish, sums)
    gtok_ref[...] = sums[:rows].astype(BF16)
    att_ref[...] = sums[rows:].astype(BF16)
    clip_start(1)
    spread_start(0)
    spread_start(1)
    spread_forward(0)
    spread_end(0)
    spread_forward(1)
    spread_end(1)

    for dx in [0] + x_order:
        gone = [*w_across(dx), w_share(dx, 1 - yl, KS2), cot_pair(dx)]
        if dx:
            gone += [w_along(dx), w_share(dx, yl, KS1), cot_along(dx)]
            gone += [tok_along(dx, tm, KT1), tok_along(dx, pair, KT2)]
        else:
            gone += [tok_pair()]
        for one in gone:
            one.wait_send()
    for step in range(1, n_t):
        head = (tm + step) % n_t
        copy(xa1.at[head], xb1.at[tm], KB1, step, tm=head).wait_send()
        copy(xa2.at[head], xb2.at[tm], KB2, step, tm=head).wait_send()
    for d in range(1, n_z):
        cam = (z + d) % n_z
        copy(p_send.at[cam], p_all.at[z], KP, d, view=cam).wait_send()
        copy(x1.at[cam], xa1.at[z], KX1, d, view=cam).wait_send()
        copy(x2.at[cam], xa2.at[z], KX2, d, view=cam).wait_send()
    for p in range(2):
        core_copy(p).wait_send()
        for d in range(1, n_z):
            camera_copy(p, d).wait_send()
            final_copy(p, d).wait_send()
        for s in range(1, n_y):
            clip_copy(p, s).wait_send()
        for d in range(n_z):
            final_share(p, d).wait_send()


def shards(n_d, n_z, n_t, tokens, cotangent, w_query, w_key, w_value, w_out, masks, rig_ids):
    rows, width = tokens.shape[2], tokens.shape[3]
    depth = w_query.shape[1]
    lanes = 2 * depth
    vmem = pl.BlockSpec(memory_space=pltpu.VMEM)
    smem = pl.BlockSpec(memory_space=pltpu.SMEM)
    hbm = pl.BlockSpec(memory_space=pl.ANY)
    half_block = (n_z, rows, lanes)
    most = 2 * max(n_z, n_t, n_d)
    attended, grad_rows, grads = pl.pallas_call(
        functools.partial(kernel, n_d, n_z, n_t, depth),
        out_shape=(
            jax.ShapeDtypeStruct((rows, width), BF16),
            jax.ShapeDtypeStruct((rows, width), BF16),
            jax.ShapeDtypeStruct((2 * lanes, width), F32),
        ),
        in_specs=[hbm] * 6 + [smem] * 2,
        out_specs=(vmem, vmem, vmem),
        scratch_shapes=[
            pltpu.VMEM((n_t, 2 * lanes, width), BF16),
            pltpu.VMEM((n_t, rows, width), BF16),
            pltpu.VMEM((n_t, rows, width), BF16),
            pltpu.VMEM((n_z, rows, 2 * lanes), BF16),
            pltpu.VMEM((n_z, rows, 2 * lanes), BF16),
            pltpu.VMEM((lanes, n_z * rows), BF16),
            pltpu.VMEM((n_z, n_z * rows, 2 * rows), BF16),
            pltpu.VMEM(half_block, BF16),
            pltpu.VMEM(half_block, BF16),
            pltpu.VMEM(half_block, BF16),
            pltpu.VMEM(half_block, BF16),
            pltpu.VMEM((n_t, rows, lanes), BF16),
            pltpu.VMEM((n_t, rows, lanes), BF16),
            pltpu.VMEM((2, lanes, width), F32),
            pltpu.VMEM((2, depth, width), BF16),
            pltpu.VMEM((2, depth, width), BF16),
            pltpu.VMEM((2, n_z, depth, width // n_z), BF16),
            pltpu.VMEM((2, n_z, depth, width // n_z), BF16),
            pltpu.VMEM((2, n_d // 2, depth, width // n_z), BF16),
            pltpu.VMEM((2, 2, n_z, depth, width // n_z), BF16),
            pltpu.SemaphoreType.DMA((6,)),
            pltpu.SemaphoreType.DMA((KINDS, most)),
            pltpu.SemaphoreType.DMA((KINDS, most)),
        ],
        compiler_params=pltpu.CompilerParams(
            collective_id=0, has_side_effects=True, vmem_limit_bytes=48 * 1024 * 1024
        ),
        cost_estimate=pl.CostEstimate(
            flops=3_000_000_000, bytes_accessed=8_000_000, transcendentals=1_000_000
        ),
    )(tokens.reshape(rows, width), cotangent.reshape(rows, width), w_query.T, w_key.T, w_value.T, w_out,
      masks, rig_ids)
    return (
        attended.reshape(tokens.shape),
        grad_rows.reshape(tokens.shape),
        grads[:depth].T,
        grads[lanes:lanes + depth].T,
        grads[lanes + depth:].T,
        grads[depth:lanes],
    )


def solution(mesh):
    sizes = mesh.shape
    return jax.shard_map(
        functools.partial(shards, sizes["dp"], sizes["view"], sizes["tm"]),
        mesh=mesh,
        in_specs=(
            P("dp", "view", "tm", None),
            P("dp", "view", "tm", None),
            P(None, "tm"),
            P(None, "tm"),
            P(None, "tm"),
            P("tm", None),
            P(),
            P("dp"),
        ),
        out_specs=(
            P("dp", "view", "tm", None),
            P("dp", "view", "tm", None),
            P(None, "tm"),
            P(None, "tm"),
            P(None, "tm"),
            P("tm", None),
        ),
        check_vma=False,
    )
```

time: 111 us -> 112 us (level)
  Pallas kernels: 105 us -> 101 us
  local copies, waits for them, and re-layouts: 4.67 us -> 8.61 us
    unnamed x17 -> x16, local copies, waits for them, and re-layouts: 3.69 us -> 7.63 us
    pallas_call x1, Pallas kernels: 105 us -> 101 us  [shards(): pl.pallas_call(functools.partial(kernel, n_d, n_z, n_t, depth), out_shape...]
where the time goes in v3:
time: 112 us; the launch traced here: 111 us
  Pallas kernels  101 us (90%)
  local copies, waits for them, and re-layouts  8.61 us (8%)
  between operations  1.3 us (1%)
    pallas_call x1, Pallas kernels, shards(): pl.pallas_call(functools.partial(kernel, n_d, n_z, n_t, depth), out_shape...  101 us
    unnamed x16, local copies, waits for them, and re-layouts  7.63 us

profile of v3, /device:TPU:1, one launch (start us, length us, event | category | flops | bytes accessed | tf_op | source)
XLA Modules:
  0.0 111.3 jit_solution(4279132835716275619)
XLA Ops:
  1.3 0.0 copy-start
  1.3 0.9 copy-done
  2.2 0.0 copy-start.1
  2.2 0.9 copy-done.1
  3.2 0.0 copy-start.2
  3.2 0.9 copy-done.2
  4.1 0.0 copy-start.3
  4.1 0.9 copy-done.3
  5.0 0.0 copy-start.4
  5.0 0.9 copy-done.4
  5.9 0.0 copy-start.5
  5.9 0.9 copy-done.5
  6.8 0.0 copy-start.6
  6.8 0.7 copy-done.6
  7.5 101.4 %shard_map.127 = (bf16[128,1024]{1,0:T(8,128)(2,1)S(1)}, bf16[128,1024]{1,0:T(8,128)(2,1)S(1)}, f32[256,1024]{1,0:T(8,128)S(1)}) custom-call(bf16[128,1024]{1,0:T(8,128)(2,1)S(1)} %bitcast.15, bf16[128,1024]{1,0:T(8,128)(2,1)S(1)} %bitcast.16, bf16[64,1024]{1,0:T(8,128)(2,1)S(1)} %bitcast.17, bf16[64,1024]{1,0:T(8,128)(2,1)S(1)} %bitcast.18, ...), custom_call_target="tpu_custom_call" | custom-call | flops 3000000000 | bytes 8000000 | tf_op jit(solution)/shard_map/pallas_call | solution.py:475
  109.0 1.0 fusion
  109.9 0.7 copy.17
  110.6 0.7 copy.18
Async XLA Ops:
  1.3 1.0 copy-start
  2.2 0.9 copy-start.1
  3.2 0.9 copy-start.2
  4.1 0.9 copy-start.3
  5.0 0.9 copy-start.4
  5.9 0.9 copy-start.5
  6.8 0.7 copy-start.6

commit v4 on v3

--- a/solution.py
+++ b/solution.py
@@ -11,7 +11,7 @@
 BF16 = jnp.bfloat16
 F32 = jnp.float32
 
-(KW, KV1, KV2, KS1, KS2, KT1, KT2, KC1, KC2, KP, KX1, KX2, KB1, KB2, KR, KZ, KY, KF, KG) = range(19)
+(KW, KV, KS1, KS2, KT1, KT2, KC1, KC2, KP, KQ, KX1, KX2, KB1, KB2, KR, KZ, KY, KF, KG) = range(19)
 KINDS = 19
 
 NT = (((1,), (1,)), ((), ()))
@@ -28,9 +28,9 @@
 def kernel(
     n_d, n_z, n_t, depth,
     tok_hbm, cot_hbm, wq_hbm, wk_hbm, wv_hbm, wo_hbm, masks_ref, rig_ref,
-    att_ref, gtok_ref, g_ref,
+    both_hbm, g_ref,
     w_all, tok_all, cot_all, p_send, p_all, kv_t, pairs, x1, x2, xa1, xa2, xb1, xb2,
-    g_sum, c_send, c_recv, z_send, z_recv, y_recv, fin,
+    g_sum, c_send, c_recv, z_send, z_recv, y_recv, fin, both_out,
     lsem, ssem, rsem,
 ):
     rows, width = tok_hbm.shape
@@ -66,6 +66,7 @@
     friends = [{"tm": (tm + s) % n_t} for s in range(1, n_t)]
     friends += [{"view": (z + s) % n_z} for s in range(1, n_z)]
     friends += [{"dp": (dp + 2 * s) % n_d} for s in range(1, n_y)]
+    friends += [{"view": (z + s) % n_z, "tm": pair} for s in range(1, n_z)]
     friends += [{"dp": sib}, {"dp": beyond, "tm": pair}]
     for friend in friends:
         pl.semaphore_signal(barrier, inc=1, device_id=friend, device_id_type=MESH)
@@ -79,36 +80,23 @@
     def behind(dx, side):
         return ((x - dx + n_x) % n_x) * 2 + side
 
-    half, quarter = lanes, depth
-
-    def w_rows(head, start, size):
-        return w_all.at[head, pl.ds(pl.multiple_of(start, size), size)]
-
-    def w_mine(head):
-        return w_rows(head, core * half, half)
+    def w_half(head, side):
+        return w_all.at[head, pl.ds(pl.multiple_of(side * lanes, lanes), lanes)]
 
     def w_along(dx):
-        return copy(w_mine(tm), w_mine(tm), KW, dx, tm=ahead(dx, yl))
+        return copy(w_half(tm, core), w_half(tm, core), KW, dx, tm=ahead(dx, yl))
 
     def w_across(dx):
-        head = behind(dx, yl)
-        near = w_rows(head, core * half, quarter)
-        far = w_rows(head, core * half + quarter, quarter)
-        return copy(near, near, KV1, dx, tm=pair), copy(far, far, KV2, dx, dp=beyond, tm=pair)
+        part = w_half(behind(dx, yl), core)
+        return copy(part, part, KV, dx, dp=beyond, tm=pair)
 
     def w_share(dx, side, kind):
-        part = w_mine(behind(dx, side))
+        part = w_half(behind(dx, side), core)
         return copy(part, part, kind, dx, dp=sib)
 
     def w_shared(dx, side, kind):
-        part = w_rows(behind(dx, side), (1 - core) * half, half)
+        part = w_half(behind(dx, side), 1 - core)
         return copy(part, part, kind, dx, dp=sib)
-
-    x_order = [1, 3, 2] if n_x == 4 else list(range(1, n_x))
-    for dx in x_order:
-        w_along(dx).start()
-    for part in w_across(0):
-        part.start()
 
     def tok_pair():
         return copy(tok_all.at[tm], tok_all.at[tm], KT1, 0, tm=pair)
@@ -123,65 +111,72 @@
     def cot_along(dx):
         return copy(cot_all.at[tm], cot_all.at[tm], KC1, dx, tm=ahead(dx, yl))
 
+    x_order = [1, 3, 2] if n_x == 4 else list(range(1, n_x))
     tok_pair().start()
+    cot_pair(0).start()
+    for dx in x_order:
+        w_along(dx).start()
 
     first = lax.broadcasted_iota(jnp.int32, (rows, lanes), 1) < depth
 
-    def project(head):
-        both = dot_nt(jnp.concatenate([tok_all[tm], cot_all[tm]], axis=0), w_all[head])
-        p_send[head, :, :lanes] = jnp.where(first, both[:rows, :lanes], both[rows:, :lanes]).astype(BF16)
-        p_send[head, :, lanes:] = both[:rows, lanes:].astype(BF16)
+    def project(head, span, place):
+        both = dot_nt(jnp.concatenate([tok_all[span], cot_all[span]], axis=0), w_all[head])
+        p_send[place, head, :, :lanes] = jnp.where(
+            first, both[:rows, :lanes], both[rows:, :lanes]
+        ).astype(BF16)
+        p_send[place, head, :, lanes:] = both[:rows, lanes:].astype(BF16)
+
+    def project_own(head):
+        project(head, tm, 0)
 
         @pl.when(head == z)
         def _():
-            p_all[z] = p_send[head]
+            p_all[z] = p_send[0, head]
 
         @pl.when(head != z)
         def _():
-            copy(p_send.at[head], p_all.at[z], KP, (head - z + n_z) % n_z, view=head).start()
-
-    project(tm)
+            copy(p_send.at[0, head], p_all.at[z], KP, (head - z + n_z) % n_z, view=head).start()
+
+    def project_pair(head):
+        project(head, pair, 1)
+        copy(
+            p_send.at[1, head], p_all.at[z], KQ, (head - z + n_z) % n_z, view=head, tm=pair
+        ).start()
+
+    project_own(tm)
     for dx in x_order:
-        copy(w_mine(behind(dx, yl)), w_mine(behind(dx, yl)), KW, dx, tm=ahead(dx, yl)).wait_recv()
-        for part in w_across(dx):
-            part.start()
+        part = w_half(behind(dx, yl), core)
+        copy(part, part, KW, dx, tm=ahead(dx, yl)).wait_recv()
         w_share(dx, yl, KS1).start()
-
     for dx in x_order:
         cot_along(dx).start()
-
-    def x_heads(i, _):
-        dx = 1 + (i + z) % (n_x - 1)
+    copy(tok_all.at[pair], tok_all.at[pair], KT1, 0, tm=pair).wait_recv()
+    copy(cot_all.at[pair], cot_all.at[pair], KC2, 0, tm=pair).wait_recv()
+    project_pair(tm)
+
+    def heads(i, _):
+        dx = 1 + (i + z // 2) % (n_x - 1)
         w_shared(dx, yl, KS1).wait_recv()
-        project(behind(dx, yl))
+        project_own(behind(dx, yl))
+        project_pair(behind(dx, yl))
         return 0
 
     if n_x > 1:
-        lax.fori_loop(0, n_x - 1, x_heads, 0)
+        lax.fori_loop(0, n_x - 1, heads, 0)
     for dx in [0] + x_order:
-        head = behind(dx, 1 - yl)
-        near = w_rows(head, core * half, quarter)
-        far = w_rows(head, core * half + quarter, quarter)
-        copy(near, near, KV1, dx, tm=pair).wait_recv()
-        copy(far, far, KV2, dx, dp=beyond, tm=pair).wait_recv()
-        w_share(dx, 1 - yl, KS2).start()
-
-    cot_pair(0).start()
-    for dx in x_order:
-        tok_along(dx, tm, KT1).start()
-
-    def y_heads(i, _):
-        dx = (i + z) % n_x
-        w_shared(dx, 1 - yl, KS2).wait_recv()
-        project(behind(dx, 1 - yl))
-        return 0
-
-    lax.fori_loop(0, n_x, y_heads, 0)
-
-    def tok_forward():
-        copy(tok_all.at[pair], tok_all.at[pair], KT1, 0, tm=pair).wait_recv()
-        for dx in x_order:
-            tok_along(dx, pair, KT2).start()
+        w_across(dx).start()
+
+    @pl.when(z % 2 == yl)
+    def _():
+        for d in range(1, n_z):
+            cam = (z - d + n_z) % n_z
+            copy(p_all.at[cam], p_all.at[cam], KP, d, view=cam).wait_recv()
+
+    @pl.when(z % 2 != yl)
+    def _():
+        for d in range(n_z):
+            cam = (z - d + n_z) % n_z
+            copy(p_all.at[cam], p_all.at[cam], KQ, d, view=cam, tm=pair).wait_recv()
 
     def cot_forward():
         for dx in x_order:
@@ -189,10 +184,6 @@
             copy(cot_all.at[span], cot_all.at[span], KC1, dx, tm=ahead(dx, yl)).wait_recv()
             cot_pair(dx).start()
 
-    for d in range(1, n_z):
-        copy(p_send.at[0], p_all.at[(z - d + n_z) % n_z], KP, d, view=(z + d) % n_z).wait_recv()
-    tok_forward()
-
     total = n_z * rows
     kv_t[...] = p_all[:, :, lanes:].reshape(total, lanes).T
     rig = rig_ref[0]
@@ -206,9 +197,16 @@
     def attend(step, _):
         cams = [(z + 1 + 2 * step) % n_z, (z + 2 + 2 * step) % n_z]
 
+        @pl.when(step == 0)
+        def _():
+            cot_forward()
+            for dx in x_order:
+                tok_along(dx, tm, KT1).start()
+
         @pl.when(step == 1)
         def _():
-            cot_forward()
+            for dx in x_order:
+                tok_along(dx, pair, KT2).start()
 
         query0, grad0 = split(cams[0])
         query1, grad1 = split(cams[1])
@@ -289,6 +287,11 @@
         def _():
             copy(src.at[head], dst.at[tm], kind, (head - tm + n_t) % n_t, tm=head).start()
 
+    for dx in [0] + x_order:
+        part = w_half(behind(dx, 1 - yl), core)
+        copy(part, part, KV, dx, dp=beyond, tm=pair).wait_recv()
+        w_share(dx, 1 - yl, KS2).start()
+
     def arrive1(d, _):
         head = (z - d + n_z) % n_z
 
@@ -388,7 +391,7 @@
             for cam in range(n_z):
                 place = (slice((2 * p + side) * depth, (2 * p + side + 1) * depth),
                          slice(cam * chunk, (cam + 1) * chunk))
-                g_ref[place] = fin[p, side, cam].astype(F32)
+                g_ref[place] = fin[p, side, cam]
 
     def finish(head, sums):
         one, two = xa1[head], xa2[head]
@@ -406,7 +409,7 @@
         span, other = behind(dx, yl), behind(dx, 1 - yl)
         copy(tok_all.at[span], tok_all.at[span], KT1, dx, tm=ahead(dx, yl)).wait_recv()
         copy(tok_all.at[other], tok_all.at[other], KT2, dx, tm=ahead(dx, yl)).wait_recv()
-    for dx in [0] + x_order:
+    for dx in x_order:
         other = behind(dx, 1 - yl)
         copy(cot_all.at[other], cot_all.at[other], KC2, dx, tm=pair).wait_recv()
     tokens = tok_all[...].reshape(n_t * rows, width)
@@ -421,11 +424,14 @@
     camera_start(0)
     core_start(1)
     camera_start(1)
+    for dx in [0] + x_order:
+        w_shared(dx, 1 - yl, KS2).wait_recv()
     sums = lax.fori_loop(0, n_z // 2, finish, jnp.zeros((2 * rows, width), F32))
     clip_start(0)
     sums = lax.fori_loop(n_z // 2, n_z, finish, sums)
-    gtok_ref[...] = sums[:rows].astype(BF16)
-    att_ref[...] = sums[rows:].astype(BF16)
+    both_out[...] = sums.astype(BF16)
+    store = pltpu.make_async_copy(both_out, both_hbm, lsem.at[6])
+    store.start()
     clip_start(1)
     spread_start(0)
     spread_start(1)
@@ -434,8 +440,9 @@
     spread_forward(1)
     spread_end(1)
 
+    store.wait()
     for dx in [0] + x_order:
-        gone = [*w_across(dx), w_share(dx, 1 - yl, KS2), cot_pair(dx)]
+        gone = [w_across(dx), w_share(dx, 1 - yl, KS2), cot_pair(dx)]
         if dx:
             gone += [w_along(dx), w_share(dx, yl, KS1), cot_along(dx)]
             gone += [tok_along(dx, tm, KT1), tok_along(dx, pair, KT2)]
@@ -449,9 +456,17 @@
         copy(xa2.at[head], xb2.at[tm], KB2, step, tm=head).wait_send()
     for d in range(1, n_z):
         cam = (z + d) % n_z
-        copy(p_send.at[cam], p_all.at[z], KP, d, view=cam).wait_send()
         copy(x1.at[cam], xa1.at[z], KX1, d, view=cam).wait_send()
         copy(x2.at[cam], xa2.at[z], KX2, d, view=cam).wait_send()
+    for dx in range(n_x):
+        head = behind(dx, yl)
+        d = (head - z + n_z) % n_z
+        copy(p_send.at[1, head], p_all.at[z], KQ, d, view=head, tm=pair).wait_send()
+
+        @pl.when(head != z)
+        def _():
+            copy(p_send.at[0, head], p_all.at[z], KP, d, view=head).wait_send()
+
     for p in range(2):
         core_copy(p).wait_send()
         for d in range(1, n_z):
@@ -469,23 +484,22 @@
     lanes = 2 * depth
     vmem = pl.BlockSpec(memory_space=pltpu.VMEM)
     smem = pl.BlockSpec(memory_space=pltpu.SMEM)
-    hbm = pl.BlockSpec(memory_space=pl.ANY)
+    hbm = pl.BlockSpec(memory_space=pltpu.HBM)
     half_block = (n_z, rows, lanes)
     most = 2 * max(n_z, n_t, n_d)
-    attended, grad_rows, grads = pl.pallas_call(
+    both, grads = pl.pallas_call(
         functools.partial(kernel, n_d, n_z, n_t, depth),
         out_shape=(
-            jax.ShapeDtypeStruct((rows, width), BF16),
-            jax.ShapeDtypeStruct((rows, width), BF16),
-            jax.ShapeDtypeStruct((2 * lanes, width), F32),
+            jax.ShapeDtypeStruct((2 * rows, width), BF16),
+            jax.ShapeDtypeStruct((2 * lanes, width), BF16),
         ),
         in_specs=[hbm] * 6 + [smem] * 2,
-        out_specs=(vmem, vmem, vmem),
+        out_specs=(hbm, vmem),
         scratch_shapes=[
             pltpu.VMEM((n_t, 2 * lanes, width), BF16),
             pltpu.VMEM((n_t, rows, width), BF16),
             pltpu.VMEM((n_t, rows, width), BF16),
-            pltpu.VMEM((n_z, rows, 2 * lanes), BF16),
+            pltpu.VMEM((2, n_t, rows, 2 * lanes), BF16),
             pltpu.VMEM((n_z, rows, 2 * lanes), BF16),
             pltpu.VMEM((lanes, n_z * rows), BF16),
             pltpu.VMEM((n_z, n_z * rows, 2 * rows), BF16),
@@ -502,21 +516,23 @@
             pltpu.VMEM((2, n_z, depth, width // n_z), BF16),
             pltpu.VMEM((2, n_d // 2, depth, width // n_z), BF16),
             pltpu.VMEM((2, 2, n_z, depth, width // n_z), BF16),
-            pltpu.SemaphoreType.DMA((6,)),
+            pltpu.VMEM((2 * rows, width), BF16),
+            pltpu.SemaphoreType.DMA((7,)),
             pltpu.SemaphoreType.DMA((KINDS, most)),
             pltpu.SemaphoreType.DMA((KINDS, most)),
         ],
         compiler_params=pltpu.CompilerParams(
-            collective_id=0, has_side_effects=True, vmem_limit_bytes=48 * 1024 * 1024
+            collective_id=0, has_side_effects=True, vmem_limit_bytes=60 * 1024 * 1024
         ),
         cost_estimate=pl.CostEstimate(
             flops=3_000_000_000, bytes_accessed=8_000_000, transcendentals=1_000_000
         ),
     )(tokens.reshape(rows, width), cotangent.reshape(rows, width), w_query.T, w_key.T, w_value.T, w_out,
       masks, rig_ids)
+    grads = grads.astype(F32)
     return (
-        attended.reshape(tokens.shape),
-        grad_rows.reshape(tokens.shape),
+        both[rows:].reshape(tokens.shape),
+        both[:rows].reshape(tokens.shape),
         grads[:depth].T,
         grads[lanes:lanes + depth].T,
         grads[lanes + depth:].T,

time: 112 us -> 113 us (level)
  Pallas kernels: 101 us -> 108 us
  local copies, waits for them, and re-layouts: 8.61 us -> 3.53 us
    unnamed x16 -> x2, local copies, waits for them, and re-layouts: 7.63 us -> 0.01 us
    pallas_call x1, Pallas kernels: 101 us -> 108 us  [shards(): pl.pallas_call(functools.partial(kernel, n_d, n_z, n_t, depth), out_shape...]
    reshape x0 -> x1, local copies, waits for them, and re-layouts: none -> 1.91 us  [shards(): both[:rows].reshape(tokens.shape)]
where the time goes in v4:
time: 113 us; the launch traced here: 112 us
  Pallas kernels  108 us (96%)
  local copies, waits for them, and re-layouts  3.53 us (3%)
  between operations  1.31 us (1%)
    pallas_call x1, Pallas kernels, shards(): pl.pallas_call(functools.partial(kernel, n_d, n_z, n_t, depth), out_shape...  108 us

profile of v4, /device:TPU:1, one launch (start us, length us, event | category | flops | bytes accessed | tf_op | source)
XLA Modules:
  0.0 112.5 jit_solution(9241457533775324574)
XLA Ops:
  1.3 107.6 %shard_map.127 = (bf16[256,1024]{1,0:T(8,128)(2,1)}, bf16[256,1024]{1,0:T(8,128)(2,1)}) custom-call(bf16[128,1024]{1,0:T(8,128)(2,1)} %bitcast.15, bf16[128,1024]{1,0:T(8,128)(2,1)} %bitcast.16, bf16[64,1024]{1,0:T(8,128)(2,1)} %bitcast.17, bf16[64,1024]{1,0:T(8,128)(2,1)} %bitcast.18, bf16[64,1024]{1,0:T(8,128)(2,1)} %bitcast.19, bf16[64,1024]{1,0:T(8,128)(2,1)} %wo_hbm.1, ...), custom_call_target="tpu_custom_call" | custom-call | flops 3000000000 | bytes 8000000 | tf_op jit(solution)/shard_map/pallas_call | solution.py:490
  108.8 0.0 copy-start
  108.9 1.9 %slice_bitcast_fusion.3 = (bf16[1,1,128,1024]{3,2,1,0:T(8,128)(2,1)}, bf16[1,1,128,1024]{3,2,1,0:T(8,128)(2,1)}) fusion(bf16[256,1024]{1,0:T(8,128)(2,1)} %get-tuple-element.8), kind=kLoop, calls=%fused_computation.3 | loop fusion | bytes 1048576 | tf_op jit(solution)/shard_map/reshape | solution.py:535
  110.8 0.0 copy-done
  110.8 0.7 slice.27
  111.5 0.1 convert_element_type.3
  111.6 0.9 slice_bitcast_fusion
Async XLA Ops:
  108.8 1.9 %copy-start = (bf16[256,1024]{1,0:T(8,128)(2,1)S(1)}, bf16[256,1024]{1,0:T(8,128)(2,1)}, u32[]{:S(2)}) copy-start(bf16[256,1024]{1,0:T(8,128)(2,1)} %get-tuple-element.9) | copy-start | bytes 1572868

commit v5 on v3

--- a/solution.py
+++ b/solution.py
@@ -11,8 +11,9 @@
 BF16 = jnp.bfloat16
 F32 = jnp.float32
 
-(KW, KV1, KV2, KS1, KS2, KT1, KT2, KC1, KC2, KP, KX1, KX2, KB1, KB2, KR, KZ, KY, KF, KG) = range(19)
-KINDS = 19
+(KW, KV1, KV2, KS1, KS2, KT1, KT2, KC1, KC2, KP, KX1, KX2, KB1, KB2, KR, KZ, KY, KF, KG) = (
+    *range(14), 14, 16, 18, 20, 22)
+KINDS = 24
 
 NT = (((1,), (1,)), ((), ()))
 
@@ -23,14 +24,21 @@
 
 def dot_nt(a, b):
     return lax.dot_general(a, b, NT, preferred_element_type=F32)
+
+
+def receive_places(n_d, n_z, n_t):
+    n_x = n_t // 2
+    sizes = [n_x] * 9 + [1, n_z, n_z, 1, 1] + [1] * 6 + [n_z] * 2 + [1] * 2
+    starts = [(sum(sizes[:k]), sizes[k]) for k in range(KINDS)]
+    return starts, sum(sizes)
 
 
 def kernel(
     n_d, n_z, n_t, depth,
     tok_hbm, cot_hbm, wq_hbm, wk_hbm, wv_hbm, wo_hbm, masks_ref, rig_ref,
-    att_ref, gtok_ref, g_ref,
+    att_hbm, gtok_hbm, g_hbm,
     w_all, tok_all, cot_all, p_send, p_all, kv_t, pairs, x1, x2, xa1, xa2, xb1, xb2,
-    g_sum, c_send, c_recv, z_send, z_recv, y_recv, fin,
+    g_sum, c_send, c_recv, z_send, z_recv, y_recv, fin, both_out, g_out,
     lsem, ssem, rsem,
 ):
     rows, width = tok_hbm.shape
@@ -56,11 +64,26 @@
     for load in loads:
         load.start()
 
+    starts, _ = receive_places(n_d, n_z, n_t)
+
     def copy(src, dst, kind, at, **to):
+        start, size = starts[kind]
+        place = start + at if size > 1 else start
         return pltpu.make_async_remote_copy(
-            src_ref=src, dst_ref=dst, send_sem=ssem.at[kind, at], recv_sem=rsem.at[kind, at],
+            src_ref=src, dst_ref=dst, send_sem=ssem.at[kind], recv_sem=rsem.at[place],
             device_id=to, device_id_type=MESH,
         )
+
+    def arrived(kind, ref):
+        copy(ref, ref, kind, 0, dp=sib).wait_recv()
+
+    def gone(kind, ref):
+        copy(ref, ref, kind, 0, dp=sib).wait_send()
+
+    def blocks(halves):
+        if halves % 2:
+            return tok_all.at[0, pl.ds(0, rows // 2)]
+        return tok_all.at[pl.ds(0, halves // 2)]
 
     barrier = pltpu.get_barrier_semaphore()
     friends = [{"tm": (tm + s) % n_t} for s in range(1, n_t)]
@@ -104,8 +127,10 @@
         part = w_rows(behind(dx, side), (1 - core) * half, half)
         return copy(part, part, kind, dx, dp=sib)
 
-    x_order = [1, 3, 2] if n_x == 4 else list(range(1, n_x))
-    for dx in x_order:
+    x_near = [1, 3] if n_x == 4 else list(range(1, n_x))
+    x_far = [2] if n_x == 4 else []
+    x_order = x_near + x_far
+    for dx in x_near:
         w_along(dx).start()
     for part in w_across(0):
         part.start()
@@ -122,8 +147,6 @@
 
     def cot_along(dx):
         return copy(cot_all.at[tm], cot_all.at[tm], KC1, dx, tm=ahead(dx, yl))
-
-    tok_pair().start()
 
     first = lax.broadcasted_iota(jnp.int32, (rows, lanes), 1) < depth
 
@@ -140,25 +163,14 @@
         def _():
             copy(p_send.at[head], p_all.at[z], KP, (head - z + n_z) % n_z, view=head).start()
 
-    project(tm)
-    for dx in x_order:
-        copy(w_mine(behind(dx, yl)), w_mine(behind(dx, yl)), KW, dx, tm=ahead(dx, yl)).wait_recv()
-        for part in w_across(dx):
-            part.start()
+    def w_arrive(dx):
+        part = w_mine(behind(dx, yl))
+        copy(part, part, KW, dx, tm=ahead(dx, yl)).wait_recv()
+        for piece in w_across(dx):
+            piece.start()
         w_share(dx, yl, KS1).start()
 
-    for dx in x_order:
-        cot_along(dx).start()
-
-    def x_heads(i, _):
-        dx = 1 + (i + z) % (n_x - 1)
-        w_shared(dx, yl, KS1).wait_recv()
-        project(behind(dx, yl))
-        return 0
-
-    if n_x > 1:
-        lax.fori_loop(0, n_x - 1, x_heads, 0)
-    for dx in [0] + x_order:
+    def w_arrive_across(dx):
         head = behind(dx, 1 - yl)
         near = w_rows(head, core * half, quarter)
         far = w_rows(head, core * half + quarter, quarter)
@@ -166,22 +178,37 @@
         copy(far, far, KV2, dx, dp=beyond, tm=pair).wait_recv()
         w_share(dx, 1 - yl, KS2).start()
 
+    def project_side(dxs, side, kind):
+        def one(i, _):
+            dx = dxs[0] + 2 * ((i + z) % len(dxs))
+            w_shared(dx, side, kind).wait_recv()
+            project(behind(dx, side))
+            return 0
+
+        if dxs:
+            lax.fori_loop(0, len(dxs), one, 0)
+
+    project(tm)
+    w_arrive_across(0)
+    for dx in x_near:
+        w_arrive(dx)
+    for dx in x_far:
+        w_along(dx).start()
+    project_side([0], 1 - yl, KS2)
+    project_side(x_near, yl, KS1)
+    for dx in x_near:
+        w_arrive_across(dx)
+    project_side(x_near, 1 - yl, KS2)
+    for dx in x_far:
+        w_arrive(dx)
+    for dx in x_order:
+        cot_along(dx).start()
+    project_side(x_far, yl, KS1)
+    for dx in x_far:
+        w_arrive_across(dx)
+    tok_pair().start()
     cot_pair(0).start()
-    for dx in x_order:
-        tok_along(dx, tm, KT1).start()
-
-    def y_heads(i, _):
-        dx = (i + z) % n_x
-        w_shared(dx, 1 - yl, KS2).wait_recv()
-        project(behind(dx, 1 - yl))
-        return 0
-
-    lax.fori_loop(0, n_x, y_heads, 0)
-
-    def tok_forward():
-        copy(tok_all.at[pair], tok_all.at[pair], KT1, 0, tm=pair).wait_recv()
-        for dx in x_order:
-            tok_along(dx, pair, KT2).start()
+    project_side(x_far, 1 - yl, KS2)
 
     def cot_forward():
         for dx in x_order:
@@ -189,9 +216,7 @@
             copy(cot_all.at[span], cot_all.at[span], KC1, dx, tm=ahead(dx, yl)).wait_recv()
             cot_pair(dx).start()
 
-    for d in range(1, n_z):
-        copy(p_send.at[0], p_all.at[(z - d + n_z) % n_z], KP, d, view=(z + d) % n_z).wait_recv()
-    tok_forward()
+    arrived(KP, p_send.at[pl.ds(0, n_z - 1)])
 
     total = n_z * rows
     kv_t[...] = p_all[:, :, lanes:].reshape(total, lanes).T
@@ -206,9 +231,17 @@
     def attend(step, _):
         cams = [(z + 1 + 2 * step) % n_z, (z + 2 + 2 * step) % n_z]
 
+        @pl.when(step == 0)
+        def _():
+            cot_forward()
+            for dx in x_order:
+                tok_along(dx, tm, KT1).start()
+
         @pl.when(step == 1)
         def _():
-            cot_forward()
+            copy(tok_all.at[pair], tok_all.at[pair], KT1, 0, tm=pair).wait_recv()
+            for dx in x_order:
+                tok_along(dx, pair, KT2).start()
 
         query0, grad0 = split(cams[0])
         query1, grad1 = split(cams[1])
@@ -312,33 +345,28 @@
     lax.fori_loop(0, n_z, lambda i, _: arrive1((i + tm) % n_z, _), 0)
     lax.fori_loop(0, n_z, lambda i, _: arrive2((i + tm) % n_z, _), 0)
 
-    def handed(ref, kind):
-        for f in range(1, n_t):
-            span = (tm - f + n_t) % n_t
-            copy(ref.at[span], ref.at[span], kind, f, tm=span).wait_recv()
-
     chunk = width // n_z
     keep = pl.multiple_of(core * depth, depth)
     give = pl.multiple_of((1 - core) * depth, depth)
 
     def core_copy(p):
-        return copy(c_send.at[p], c_recv.at[p], KR, p, dp=sib)
+        return copy(c_send.at[p], c_recv.at[p], KR + p, 0, dp=sib)
 
     def camera_copy(p, d):
         cam = (z + d) % n_z
-        return copy(z_send.at[p, cam], z_recv.at[p, z], KZ, p * n_z + d, view=cam)
+        return copy(z_send.at[p, cam], z_recv.at[p, z], KZ + p, d, view=cam)
 
     def clip_copy(p, s):
         part = y_recv.at[p, yh]
-        return copy(part, part, KY, p * n_y + s, dp=(dp + 2 * s) % n_d)
+        return copy(part, part, KY + p, s, dp=(dp + 2 * s) % n_d)
 
     def final_copy(p, d):
         part = fin.at[p, core, z]
-        return copy(part, part, KF, p * n_z + d, view=(z + d) % n_z)
+        return copy(part, part, KF + p, d, view=(z + d) % n_z)
 
     def final_share(p, d):
         part = fin.at[p, core, (z - d + n_z) % n_z]
-        return copy(part, part, KG, p * n_z + d, dp=sib)
+        return copy(part, part, KG + p, d, dp=sib)
 
     def core_start(p):
         c_send[p] = g_sum[p, pl.ds(give, depth)].astype(BF16)
@@ -354,18 +382,16 @@
 
     def clip_start(p):
         total = z_send[p, z].astype(F32)
+        arrived(KZ + p, z_recv.at[p, pl.ds(0, n_z - 1)])
         for d in range(1, n_z):
-            cam = (z - d + n_z) % n_z
-            copy(z_recv.at[p, cam], z_recv.at[p, cam], KZ, p * n_z + d, view=cam).wait_recv()
-            total = total + z_recv[p, cam].astype(F32)
+            total = total + z_recv[p, (z - d + n_z) % n_z].astype(F32)
         y_recv[p, yh] = total.astype(BF16)
         for s in range(1, n_y):
             clip_copy(p, s).start()
 
     def spread_start(p):
-        for s in range(1, n_y):
-            other = y_recv.at[p, (yh - s + n_y) % n_y]
-            copy(other, other, KY, p * n_y + s, dp=(dp + 2 * s) % n_d).wait_recv()
+        if n_y > 1:
+            arrived(KY + p, y_recv.at[p, pl.ds(0, n_y - 1)])
         total = y_recv[p, 0].astype(F32)
         for s in range(1, n_y):
             total = total + y_recv[p, s].astype(F32)
@@ -377,18 +403,21 @@
     def spread_forward(p):
         for d in range(1, n_z):
             part = fin.at[p, core, (z - d + n_z) % n_z]
-            copy(part, part, KF, p * n_z + d, view=(z + d) % n_z).wait_recv()
+            copy(part, part, KF + p, d, view=(z + d) % n_z).wait_recv()
             final_share(p, d).start()
 
     def spread_end(p):
-        for d in range(n_z):
-            part = fin.at[p, 1 - core, (z - d + n_z) % n_z]
-            copy(part, part, KG, p * n_z + d, dp=sib).wait_recv()
+        arrived(KG + p, fin.at[p, 1 - core])
         for side in range(2):
             for cam in range(n_z):
                 place = (slice((2 * p + side) * depth, (2 * p + side + 1) * depth),
                          slice(cam * chunk, (cam + 1) * chunk))
-                g_ref[place] = fin[p, side, cam].astype(F32)
+                g_out[place] = fin[p, side, cam].astype(F32)
+        return g_store(p)
+
+    def g_store(p):
+        part = pl.ds(p * lanes, lanes)
+        return pltpu.make_async_copy(g_out.at[part], g_hbm.at[part], lsem.at[8 + p])
 
     def finish(head, sums):
         one, two = xa1[head], xa2[head]
@@ -411,12 +440,12 @@
         copy(cot_all.at[other], cot_all.at[other], KC2, dx, tm=pair).wait_recv()
     tokens = tok_all[...].reshape(n_t * rows, width)
     cots = cot_all[...].reshape(n_t * rows, width)
-    handed(xb1, KB1)
+    arrived(KB1, xb1.at[pl.ds(0, n_t - 1)])
     b1 = xb1[...].reshape(n_t * rows, lanes).T
     g_sum[0, :depth] = dot(b1[:depth], tokens)
     g_sum[0, depth:] = dot(b1[depth:], cots)
     core_start(0)
-    handed(xb2, KB2)
+    arrived(KB2, xb2.at[pl.ds(0, n_t - 1)])
     g_sum[1] = dot(xb2[...].reshape(n_t * rows, lanes).T, tokens)
     camera_start(0)
     core_start(1)
@@ -424,54 +453,56 @@
     sums = lax.fori_loop(0, n_z // 2, finish, jnp.zeros((2 * rows, width), F32))
     clip_start(0)
     sums = lax.fori_loop(n_z // 2, n_z, finish, sums)
-    gtok_ref[...] = sums[:rows].astype(BF16)
-    att_ref[...] = sums[rows:].astype(BF16)
+    both_out[...] = sums.astype(BF16)
+    stores = [
+        pltpu.make_async_copy(both_out.at[pl.ds(0, rows)], gtok_hbm, lsem.at[6]),
+        pltpu.make_async_copy(both_out.at[pl.ds(rows, rows)], att_hbm, lsem.at[7]),
+    ]
+    for store in stores:
+        store.start()
     clip_start(1)
     spread_start(0)
     spread_start(1)
     spread_forward(0)
-    spread_end(0)
+    stores.append(spread_end(0))
+    stores[-1].start()
     spread_forward(1)
-    spread_end(1)
-
-    for dx in [0] + x_order:
-        gone = [*w_across(dx), w_share(dx, 1 - yl, KS2), cot_pair(dx)]
-        if dx:
-            gone += [w_along(dx), w_share(dx, yl, KS1), cot_along(dx)]
-            gone += [tok_along(dx, tm, KT1), tok_along(dx, pair, KT2)]
-        else:
-            gone += [tok_pair()]
-        for one in gone:
-            one.wait_send()
-    for step in range(1, n_t):
-        head = (tm + step) % n_t
-        copy(xa1.at[head], xb1.at[tm], KB1, step, tm=head).wait_send()
-        copy(xa2.at[head], xb2.at[tm], KB2, step, tm=head).wait_send()
-    for d in range(1, n_z):
-        cam = (z + d) % n_z
-        copy(p_send.at[cam], p_all.at[z], KP, d, view=cam).wait_send()
-        copy(x1.at[cam], xa1.at[z], KX1, d, view=cam).wait_send()
-        copy(x2.at[cam], xa2.at[z], KX2, d, view=cam).wait_send()
+    stores.append(spread_end(1))
+    stores[-1].start()
+
+    far_units = n_x - 1
+    gone(KV1, blocks(n_x))
+    gone(KV2, blocks(n_x))
+    gone(KS2, blocks(2 * n_x))
+    gone(KC2, blocks(2 * n_x))
+    gone(KT1, blocks(2 * n_x))
+    if far_units:
+        for kind in (KW, KS1, KT2, KC1):
+            gone(kind, blocks(2 * far_units))
+    gone(KP, p_send.at[pl.ds(0, n_z - 1)])
+    gone(KX1, x1.at[pl.ds(0, n_z - 1)])
+    gone(KX2, x2.at[pl.ds(0, n_z - 1)])
+    gone(KB1, xb1.at[pl.ds(0, n_t - 1)])
+    gone(KB2, xb2.at[pl.ds(0, n_t - 1)])
     for p in range(2):
-        core_copy(p).wait_send()
-        for d in range(1, n_z):
-            camera_copy(p, d).wait_send()
-            final_copy(p, d).wait_send()
-        for s in range(1, n_y):
-            clip_copy(p, s).wait_send()
-        for d in range(n_z):
-            final_share(p, d).wait_send()
+        gone(KR + p, c_send.at[p])
+        gone(KZ + p, z_send.at[p, pl.ds(0, n_z - 1)])
+        if n_y > 1:
+            gone(KY + p, y_recv.at[p, pl.ds(0, n_y - 1)])
+        gone(KF + p, fin.at[p, 0, pl.ds(0, n_z - 1)])
+        gone(KG + p, fin.at[p, 0])
+    for store in stores:
+        store.wait()
 
 
 def shards(n_d, n_z, n_t, tokens, cotangent, w_query, w_key, w_value, w_out, masks, rig_ids):
     rows, width = tokens.shape[2], tokens.shape[3]
     depth = w_query.shape[1]
     lanes = 2 * depth
-    vmem = pl.BlockSpec(memory_space=pltpu.VMEM)
     smem = pl.BlockSpec(memory_space=pltpu.SMEM)
-    hbm = pl.BlockSpec(memory_space=pl.ANY)
+    hbm = pl.BlockSpec(memory_space=pltpu.HBM)
     half_block = (n_z, rows, lanes)
-    most = 2 * max(n_z, n_t, n_d)
+    _, places = receive_places(n_d, n_z, n_t)
     attended, grad_rows, grads = pl.pallas_call(
         functools.partial(kernel, n_d, n_z, n_t, depth),
         out_shape=(
@@ -480,7 +511,7 @@
             jax.ShapeDtypeStruct((2 * lanes, width), F32),
         ),
         in_specs=[hbm] * 6 + [smem] * 2,
-        out_specs=(vmem, vmem, vmem),
+        out_specs=(hbm, hbm, hbm),
         scratch_shapes=[
             pltpu.VMEM((n_t, 2 * lanes, width), BF16),
             pltpu.VMEM((n_t, rows, width), BF16),
@@ -502,12 +533,14 @@
             pltpu.VMEM((2, n_z, depth, width // n_z), BF16),
             pltpu.VMEM((2, n_d // 2, depth, width // n_z), BF16),
             pltpu.VMEM((2, 2, n_z, depth, width // n_z), BF16),
-            pltpu.SemaphoreType.DMA((6,)),
-            pltpu.SemaphoreType.DMA((KINDS, most)),
-            pltpu.SemaphoreType.DMA((KINDS, most)),
+            pltpu.VMEM((2 * rows, width), BF16),
+            pltpu.VMEM((2 * lanes, width), F32),
+            pltpu.SemaphoreType.DMA((10,)),
+            pltpu.SemaphoreType.DMA((KINDS,)),
+            pltpu.SemaphoreType.DMA((places,)),
         ],
         compiler_params=pltpu.CompilerParams(
-            collective_id=0, has_side_effects=True, vmem_limit_bytes=48 * 1024 * 1024
+            collective_id=0, has_side_effects=True, vmem_limit_bytes=60 * 1024 * 1024
         ),
         cost_estimate=pl.CostEstimate(
             flops=3_000_000_000, bytes_accessed=8_000_000, transcendentals=1_000_000

time: 112 us -> 106 us (0.946)
  local copies, waits for them, and re-layouts: 8.61 us -> 3.96 us
    unnamed x16 -> x6, local copies, waits for them, and re-layouts: 7.63 us -> 1.75 us
    pallas_call x1, Pallas kernels: 101 us -> 100 us  [shards(): pl.pallas_call(functools.partial(kernel, n_d, n_z, n_t, depth), out_shape...]
    slice x1, local copies, waits for them, and re-layouts: 0.98 us -> 2.21 us  [shards(): grads[depth:lanes]]
where the time goes in v5:
time: 106 us; the launch traced here: 105 us
  Pallas kernels  100 us (94%)
  local copies, waits for them, and re-layouts  3.96 us (4%)
  between operations  1.3 us (1%)
    pallas_call x1, Pallas kernels, shards(): pl.pallas_call(functools.partial(kernel, n_d, n_z, n_t, depth), out_shape...  100 us
    slice x1, local copies, waits for them, and re-layouts, shards(): grads[depth:lanes]  2.21 us

profile of v5, /device:TPU:1, one launch (start us, length us, event | category | flops | bytes accessed | tf_op | source)
XLA Modules:
  0.0 105.5 jit_solution(17060250191834027352)
XLA Ops:
  1.3 100.2 %shard_map.127 = (bf16[128,1024]{1,0:T(8,128)(2,1)}, bf16[128,1024]{1,0:T(8,128)(2,1)}, f32[256,1024]{1,0:T(8,128)}) custom-call(bf16[128,1024]{1,0:T(8,128)(2,1)} %bitcast.15, bf16[128,1024]{1,0:T(8,128)(2,1)} %bitcast.16, bf16[64,1024]{1,0:T(8,128)(2,1)} %bitcast.17, bf16[64,1024]{1,0:T(8,128)(2,1)} %bitcast.18, bf16[64,1024]{1,0:T(8,128)(2,1)} %bitcast.19, ...), custom_call_target="tpu_custom_call" | custom-call | flops 3000000000 | bytes 8000000 | tf_op jit(solution)/shard_map/pallas_call | solution.py:506
  101.5 0.0 copy-start.1
  101.5 2.2 %fusion = (f32[64,1024]{1,0:T(8,128)}, f32[1024,64]{0,1:T(8,128)}, f32[1024,64]{0,1:T(8,128)}, f32[1024,64]{0,1:T(8,128)}) fusion(f32[256,1024]{1,0:T(8,128)} %get-tuple-element.11), kind=kLoop, calls=%fused_computation.3 | loop fusion | bytes 2097152 | tf_op jit(solution)/shard_map/slice | solution.py:556
  103.7 0.0 copy-done.1
  103.7 0.0 copy-start
  103.7 0.7 copy.17
  104.4 0.3 copy-done
  104.7 0.7 copy.18
Async XLA Ops:
  101.5 2.2 %copy-start.1 = (bf16[128,1024]{1,0:T(8,128)(2,1)S(1)}, bf16[128,1024]{1,0:T(8,128)(2,1)}, u32[]{:S(2)}) copy-start(bf16[128,1024]{1,0:T(8,128)(2,1)} %get-tuple-element.9) | copy-start | bytes 786436
  103.7 1.0 copy-start

commit v6 on v5

--- a/solution.py
+++ b/solution.py
@@ -11,9 +11,9 @@
 BF16 = jnp.bfloat16
 F32 = jnp.float32
 
-(KW, KV1, KV2, KS1, KS2, KT1, KT2, KC1, KC2, KP, KX1, KX2, KB1, KB2, KR, KZ, KY, KF, KG) = (
-    *range(14), 14, 16, 18, 20, 22)
-KINDS = 24
+(KW, KV1, KV2, KS1, KS2, KT1, KT2, KC1, KC2, KP, KX1, KX2, KB1, KB2, KR, KZ, KY, KF, KG,
+ KW2, KC3, KT3, KT4) = (*range(14), 14, 16, 18, 20, 22, *range(24, 28))
+KINDS = 28
 
 NT = (((1,), (1,)), ((), ()))
 
@@ -28,7 +28,7 @@
 
 def receive_places(n_d, n_z, n_t):
     n_x = n_t // 2
-    sizes = [n_x] * 9 + [1, n_z, n_z, 1, 1] + [1] * 6 + [n_z] * 2 + [1] * 2
+    sizes = [n_x] * 9 + [1, n_z, n_z, 1, 1] + [1] * 6 + [n_z] * 2 + [1] * 2 + [2] * 4
     starts = [(sum(sizes[:k]), sizes[k]) for k in range(KINDS)]
     return starts, sum(sizes)
 
@@ -127,6 +127,24 @@
         part = w_rows(behind(dx, side), (1 - core) * half, half)
         return copy(part, part, kind, dx, dp=sib)
 
+    relays = [(1, 1), (3, 0)]
+
+    def relay(ref, kind, side):
+        if not x_far:
+            return
+        for dx, part in relays:
+            rows_part = ref.at[behind(dx, side), pl.ds(part * (rows // 2), rows // 2)]
+            copy(rows_part, rows_part, kind, part, tm=ahead(dx, yl)).start()
+
+    def relayed(ref, kind, side):
+        for dx in x_far:
+            for part in range(2):
+                rows_part = ref.at[behind(dx, side), pl.ds(part * (rows // 2), rows // 2)]
+                copy(rows_part, rows_part, kind, part, tm=pair).wait_recv()
+
+    def w_piece(dx, part):
+        return w_rows(behind(dx, yl), core * half + part * quarter, quarter)
+
     x_near = [1, 3] if n_x == 4 else list(range(1, n_x))
     x_far = [2] if n_x == 4 else []
     x_order = x_near + x_far
@@ -164,8 +182,17 @@
             copy(p_send.at[head], p_all.at[z], KP, (head - z + n_z) % n_z, view=head).start()
 
     def w_arrive(dx):
-        part = w_mine(behind(dx, yl))
-        copy(part, part, KW, dx, tm=ahead(dx, yl)).wait_recv()
+        if dx in x_far:
+            for part in range(2):
+                piece = w_piece(dx, part)
+                copy(piece, piece, KW2, part, tm=pair).wait_recv()
+        else:
+            block = w_mine(behind(dx, yl))
+            copy(block, block, KW, dx, tm=ahead(dx, yl)).wait_recv()
+            if x_far:
+                part = dict(relays)[dx]
+                piece = w_piece(dx, part)
+                copy(piece, piece, KW2, part, tm=ahead(dx, yl)).start()
         for piece in w_across(dx):
             piece.start()
         w_share(dx, yl, KS1).start()
@@ -188,33 +215,39 @@
         if dxs:
             lax.fori_loop(0, len(dxs), one, 0)
 
+    tok_pair().start()
     project(tm)
     w_arrive_across(0)
     for dx in x_near:
         w_arrive(dx)
-    for dx in x_far:
-        w_along(dx).start()
     project_side([0], 1 - yl, KS2)
     project_side(x_near, yl, KS1)
+    for dx in x_far:
+        w_arrive(dx)
     for dx in x_near:
         w_arrive_across(dx)
+    for dx in x_near:
+        cot_along(dx).start()
+        tok_along(dx, tm, KT1).start()
     project_side(x_near, 1 - yl, KS2)
-    for dx in x_far:
-        w_arrive(dx)
-    for dx in x_order:
-        cot_along(dx).start()
     project_side(x_far, yl, KS1)
     for dx in x_far:
         w_arrive_across(dx)
-    tok_pair().start()
     cot_pair(0).start()
     project_side(x_far, 1 - yl, KS2)
 
-    def cot_forward():
-        for dx in x_order:
-            span = behind(dx, yl)
-            copy(cot_all.at[span], cot_all.at[span], KC1, dx, tm=ahead(dx, yl)).wait_recv()
-            cot_pair(dx).start()
+    for dx in x_near:
+        span = behind(dx, yl)
+        copy(cot_all.at[span], cot_all.at[span], KC1, dx, tm=pair).wait_recv()
+        cot_pair(dx).start()
+    relay(cot_all, KC3, yl)
+    for dx in x_near:
+        span = behind(dx, yl)
+        copy(tok_all.at[span], tok_all.at[span], KT1, dx, tm=pair).wait_recv()
+    relay(tok_all, KT3, yl)
+    copy(tok_all.at[pair], tok_all.at[pair], KT1, 0, tm=pair).wait_recv()
+    for dx in x_near:
+        tok_along(dx, pair, KT2).start()
 
     arrived(KP, p_send.at[pl.ds(0, n_z - 1)])
 
@@ -233,15 +266,16 @@
 
         @pl.when(step == 0)
         def _():
-            cot_forward()
-            for dx in x_order:
-                tok_along(dx, tm, KT1).start()
+            relayed(cot_all, KC3, yl)
+            for dx in x_far:
+                cot_pair(dx).start()
 
         @pl.when(step == 1)
         def _():
-            copy(tok_all.at[pair], tok_all.at[pair], KT1, 0, tm=pair).wait_recv()
-            for dx in x_order:
-                tok_along(dx, pair, KT2).start()
+            for dx in x_near:
+                span = behind(dx, 1 - yl)
+                copy(tok_all.at[span], tok_all.at[span], KT2, dx, tm=pair).wait_recv()
+            relay(tok_all, KT4, 1 - yl)
 
         query0, grad0 = split(cams[0])
         query1, grad1 = split(cams[1])
@@ -412,7 +446,7 @@
             for cam in range(n_z):
                 place = (slice((2 * p + side) * depth, (2 * p + side + 1) * depth),
                          slice(cam * chunk, (cam + 1) * chunk))
-                g_out[place] = fin[p, side, cam].astype(F32)
+                g_out[place] = fin[p, side, cam]
         return g_store(p)
 
     def g_store(p):
@@ -431,10 +465,8 @@
         )
         return sums + dot(left, w_all[head])
 
-    for dx in x_order:
-        span, other = behind(dx, yl), behind(dx, 1 - yl)
-        copy(tok_all.at[span], tok_all.at[span], KT1, dx, tm=ahead(dx, yl)).wait_recv()
-        copy(tok_all.at[other], tok_all.at[other], KT2, dx, tm=ahead(dx, yl)).wait_recv()
+    relayed(tok_all, KT3, yl)
+    relayed(tok_all, KT4, 1 - yl)
     for dx in [0] + x_order:
         other = behind(dx, 1 - yl)
         copy(cot_all.at[other], cot_all.at[other], KC2, dx, tm=pair).wait_recv()
@@ -470,15 +502,19 @@
     stores.append(spread_end(1))
     stores[-1].start()
 
-    far_units = n_x - 1
+    near = len(x_near)
     gone(KV1, blocks(n_x))
     gone(KV2, blocks(n_x))
     gone(KS2, blocks(2 * n_x))
     gone(KC2, blocks(2 * n_x))
-    gone(KT1, blocks(2 * n_x))
-    if far_units:
-        for kind in (KW, KS1, KT2, KC1):
-            gone(kind, blocks(2 * far_units))
+    gone(KT1, blocks(2 * near + 2))
+    if near:
+        for kind in (KW, KT2, KC1):
+            gone(kind, blocks(2 * near))
+        gone(KS1, blocks(2 * n_x - 2))
+    if x_far:
+        for kind in (KW2, KC3, KT3, KT4):
+            gone(kind, blocks(2))
     gone(KP, p_send.at[pl.ds(0, n_z - 1)])
     gone(KX1, x1.at[pl.ds(0, n_z - 1)])
     gone(KX2, x2.at[pl.ds(0, n_z - 1)])
@@ -508,7 +544,7 @@
         out_shape=(
             jax.ShapeDtypeStruct((rows, width), BF16),
             jax.ShapeDtypeStruct((rows, width), BF16),
-            jax.ShapeDtypeStruct((2 * lanes, width), F32),
+            jax.ShapeDtypeStruct((2 * lanes, width), BF16),
         ),
         in_specs=[hbm] * 6 + [smem] * 2,
         out_specs=(hbm, hbm, hbm),
@@ -534,7 +570,7 @@
             pltpu.VMEM((2, n_d // 2, depth, width // n_z), BF16),
             pltpu.VMEM((2, 2, n_z, depth, width // n_z), BF16),
             pltpu.VMEM((2 * rows, width), BF16),
-            pltpu.VMEM((2 * lanes, width), F32),
+            pltpu.VMEM((2 * lanes, width), BF16),
             pltpu.SemaphoreType.DMA((10,)),
             pltpu.SemaphoreType.DMA((KINDS,)),
             pltpu.SemaphoreType.DMA((places,)),
@@ -547,6 +583,7 @@
         ),
     )(tokens.reshape(rows, width), cotangent.reshape(rows, width), w_query.T, w_key.T, w_value.T, w_out,
       masks, rig_ids)
+    grads = grads.astype(F32)
     return (
         attended.reshape(tokens.shape),
         grad_rows.reshape(tokens.shape),

time: 106 us -> 103 us (0.972)
  Pallas kernels: 100 us -> 96.6 us
    pallas_call x1, Pallas kernels: 100 us -> 96.6 us  [shards(): pl.pallas_call(functools.partial(kernel, n_d, n_z, n_t, depth), out_shape...]
where the time goes in v6:
time: 103 us
  Pallas kernels  96.6 us (94%)
  local copies, waits for them, and re-layouts  4.48 us (4%)
  between operations  1.32 us (1%)
    pallas_call x1, Pallas kernels, shards(): pl.pallas_call(functools.partial(kernel, n_d, n_z, n_t, depth), out_shape...  96.6 us

profile of v6, /device:TPU:1, one launch (start us, length us, event | category | flops | bytes accessed | tf_op | source)
XLA Modules:
  0.0 102.5 jit_solution(8830411415749327726)
XLA Ops:
  1.3 96.6 %shard_map.127 = (bf16[128,1024]{1,0:T(8,128)(2,1)}, bf16[128,1024]{1,0:T(8,128)(2,1)}, bf16[256,1024]{1,0:T(8,128)(2,1)}) custom-call(bf16[128,1024]{1,0:T(8,128)(2,1)} %bitcast.15, bf16[128,1024]{1,0:T(8,128)(2,1)} %bitcast.16, bf16[64,1024]{1,0:T(8,128)(2,1)} %bitcast.17, bf16[64,1024]{1,0:T(8,128)(2,1)} %bitcast.18, bf16[64,1024]{1,0:T(8,128)(2,1)} %bitcast.19, ...), custom_call_target="tpu_custom_call" | custom-call | flops 3000000000 | bytes 8000000 | tf_op jit(solution)/shard_map/pallas_call | solution.py:542
  97.9 0.0 copy-start
  97.9 1.7 %slice.19 = f32[64,1024]{1,0:T(8,128)} slice(bf16[256,1024]{1,0:T(8,128)(2,1)} %get-tuple-element.11), slice={[64:128], [0:1024]} | slice | bytes 524288 | tf_op jit(solution)/shard_map/slice | solution.py:593
  99.6 0.0 copy-done
  99.6 0.1 convert_element_type.3
  99.7 0.0 copy-start.2
  99.8 0.9 slice_bitcast_fusion
  100.6 0.1 copy-done.2
  100.8 0.0 copy-start.1
  100.8 0.7 copy.17
  101.5 0.3 copy-done.1
  101.8 0.7 copy.18
Async XLA Ops:
  97.9 1.7 %copy-start = (bf16[256,1024]{1,0:T(8,128)(2,1)S(1)}, bf16[256,1024]{1,0:T(8,128)(2,1)}, u32[]{:S(2)}) copy-start(bf16[256,1024]{1,0:T(8,128)(2,1)} %get-tuple-element.11) | copy-start | bytes 1572868
  99.7 1.0 %copy-start.2 = (bf16[128,1024]{1,0:T(8,128)(2,1)S(1)}, bf16[128,1024]{1,0:T(8,128)(2,1)}, u32[]{:S(2)}) copy-start(bf16[128,1024]{1,0:T(8,128)(2,1)} %get-tuple-element.9) | copy-start | bytes 786436
  100.8 1.0 %copy-start.1 = (bf16[128,1024]{1,0:T(8,128)(2,1)S(1)}, bf16[128,1024]{1,0:T(8,128)(2,1)}, u32[]{:S(2)}) copy-start(bf16[128,1024]{1,0:T(8,128)(2,1)} %get-tuple-element.10) | copy-start | bytes 786436

commit v7 on v6

--- a/solution.py
+++ b/solution.py
@@ -28,7 +28,7 @@
 
 def receive_places(n_d, n_z, n_t):
     n_x = n_t // 2
-    sizes = [n_x] * 9 + [1, n_z, n_z, 1, 1] + [1] * 6 + [n_z] * 2 + [1] * 2 + [2] * 4
+    sizes = [2 * n_x] + [n_x] * 8 + [1, n_z, n_z, 1, 1] + [1] * 6 + [n_z] * 2 + [1] * 2 + [2] * 4
     starts = [(sum(sizes[:k]), sizes[k]) for k in range(KINDS)]
     return starts, sum(sizes)
 
@@ -110,14 +110,18 @@
     def w_mine(head):
         return w_rows(head, core * half, half)
 
-    def w_along(dx):
-        return copy(w_mine(tm), w_mine(tm), KW, dx, tm=ahead(dx, yl))
-
-    def w_across(dx):
-        head = behind(dx, yl)
-        near = w_rows(head, core * half, quarter)
-        far = w_rows(head, core * half + quarter, quarter)
-        return copy(near, near, KV1, dx, tm=pair), copy(far, far, KV2, dx, dp=beyond, tm=pair)
+    def pieces(dx):
+        return (1, 0) if dx == 1 else (0, 1)
+
+    def w_along(dx, part):
+        piece = w_rows(tm, core * half + part * quarter, quarter)
+        return copy(piece, piece, KW, 2 * dx + part, tm=ahead(dx, yl))
+
+    def w_across(dx, part):
+        piece = w_rows(behind(dx, yl), core * half + part * quarter, quarter)
+        if part == 0:
+            return copy(piece, piece, KV1, dx, tm=pair)
+        return copy(piece, piece, KV2, dx, dp=beyond, tm=pair)
 
     def w_share(dx, side, kind):
         part = w_mine(behind(dx, side))
@@ -148,10 +152,11 @@
     x_near = [1, 3] if n_x == 4 else list(range(1, n_x))
     x_far = [2] if n_x == 4 else []
     x_order = x_near + x_far
-    for dx in x_near:
-        w_along(dx).start()
-    for part in w_across(0):
-        part.start()
+    for turn in range(2):
+        for dx in x_near:
+            w_along(dx, pieces(dx)[turn]).start()
+    for part in range(2):
+        w_across(0, part).start()
 
     def tok_pair():
         return copy(tok_all.at[tm], tok_all.at[tm], KT1, 0, tm=pair)
@@ -181,21 +186,15 @@
         def _():
             copy(p_send.at[head], p_all.at[z], KP, (head - z + n_z) % n_z, view=head).start()
 
-    def w_arrive(dx):
+    def w_arrive(dx, part):
+        piece = w_piece(dx, part)
         if dx in x_far:
-            for part in range(2):
-                piece = w_piece(dx, part)
-                copy(piece, piece, KW2, part, tm=pair).wait_recv()
+            copy(piece, piece, KW2, part, tm=pair).wait_recv()
         else:
-            block = w_mine(behind(dx, yl))
-            copy(block, block, KW, dx, tm=ahead(dx, yl)).wait_recv()
-            if x_far:
-                part = dict(relays)[dx]
-                piece = w_piece(dx, part)
+            copy(piece, piece, KW, 2 * dx + part, tm=pair).wait_recv()
+            if x_far and part == pieces(dx)[0]:
                 copy(piece, piece, KW2, part, tm=ahead(dx, yl)).start()
-        for piece in w_across(dx):
-            piece.start()
-        w_share(dx, yl, KS1).start()
+        w_across(dx, part).start()
 
     def w_arrive_across(dx):
         head = behind(dx, 1 - yl)
@@ -218,12 +217,17 @@
     tok_pair().start()
     project(tm)
     w_arrive_across(0)
+    for turn in range(2):
+        for dx in x_near:
+            w_arrive(dx, pieces(dx)[turn])
     for dx in x_near:
-        w_arrive(dx)
+        w_share(dx, yl, KS1).start()
     project_side([0], 1 - yl, KS2)
     project_side(x_near, yl, KS1)
     for dx in x_far:
-        w_arrive(dx)
+        for part in range(2):
+            w_arrive(dx, part)
+        w_share(dx, yl, KS1).start()
     for dx in x_near:
         w_arrive_across(dx)
     for dx in x_near:
@@ -446,7 +450,7 @@
             for cam in range(n_z):
                 place = (slice((2 * p + side) * depth, (2 * p + side + 1) * depth),
                          slice(cam * chunk, (cam + 1) * chunk))
-                g_out[place] = fin[p, side, cam]
+                g_out[place] = fin[p, side, cam].astype(F32)
         return g_store(p)
 
     def g_store(p):
@@ -544,7 +548,7 @@
         out_shape=(
             jax.ShapeDtypeStruct((rows, width), BF16),
             jax.ShapeDtypeStruct((rows, width), BF16),
-            jax.ShapeDtypeStruct((2 * lanes, width), BF16),
+            jax.ShapeDtypeStruct((2 * lanes, width), F32),
         ),
         in_specs=[hbm] * 6 + [smem] * 2,
         out_specs=(hbm, hbm, hbm),
@@ -570,7 +574,7 @@
             pltpu.VMEM((2, n_d // 2, depth, width // n_z), BF16),
             pltpu.VMEM((2, 2, n_z, depth, width // n_z), BF16),
             pltpu.VMEM((2 * rows, width), BF16),
-            pltpu.VMEM((2 * lanes, width), BF16),
+            pltpu.VMEM((2 * lanes, width), F32),
             pltpu.SemaphoreType.DMA((10,)),
             pltpu.SemaphoreType.DMA((KINDS,)),
             pltpu.SemaphoreType.DMA((places,)),
@@ -583,7 +587,6 @@
         ),
     )(tokens.reshape(rows, width), cotangent.reshape(rows, width), w_query.T, w_key.T, w_value.T, w_out,
       masks, rig_ids)
-    grads = grads.astype(F32)
     return (
         attended.reshape(tokens.shape),
         grad_rows.reshape(tokens.shape),

time: 103 us -> 102 us (level)
  no operation moved by 1% of the time
where the time goes in v7:
time: 102 us
  Pallas kernels  96.7 us (95%)
  local copies, waits for them, and re-layouts  3.96 us (4%)
  between operations  1.3 us (1%)
    pallas_call x1, Pallas kernels, shards(): pl.pallas_call(functools.partial(kernel, n_d, n_z, n_t, depth), out_shape...  96.7 us
    slice x1, local copies, waits for them, and re-layouts, shards(): grads[depth:lanes]  2.21 us

profile of v7, /device:TPU:1, one launch (start us, length us, event | category | flops | bytes accessed | tf_op | source)
XLA Modules:
  0.0 101.9 jit_solution(2913560287882966334)
XLA Ops:
  1.3 96.7 %shard_map.127 = (bf16[128,1024]{1,0:T(8,128)(2,1)}, bf16[128,1024]{1,0:T(8,128)(2,1)}, f32[256,1024]{1,0:T(8,128)}) custom-call(bf16[128,1024]{1,0:T(8,128)(2,1)} %bitcast.15, bf16[128,1024]{1,0:T(8,128)(2,1)} %bitcast.16, bf16[64,1024]{1,0:T(8,128)(2,1)} %bitcast.17, bf16[64,1024]{1,0:T(8,128)(2,1)} %bitcast.18, bf16[64,1024]{1,0:T(8,128)(2,1)} %bitcast.19, ...), custom_call_target="tpu_custom_call" | custom-call | flops 3000000000 | bytes 8000000 | tf_op jit(solution)/shard_map/pallas_call | solution.py:546
  97.9 0.0 copy-start.1
  98.0 2.2 %fusion = (f32[64,1024]{1,0:T(8,128)}, f32[1024,64]{0,1:T(8,128)}, f32[1024,64]{0,1:T(8,128)}, f32[1024,64]{0,1:T(8,128)}) fusion(f32[256,1024]{1,0:T(8,128)} %get-tuple-element.11), kind=kLoop, calls=%fused_computation.3 | loop fusion | bytes 2097152 | tf_op jit(solution)/shard_map/slice | solution.py:596
  100.2 0.0 copy-done.1
  100.2 0.0 copy-start
  100.2 0.7 copy.17
  100.9 0.3 copy-done
  101.2 0.7 copy.18
Async XLA Ops:
  97.9 2.2 %copy-start.1 = (bf16[128,1024]{1,0:T(8,128)(2,1)S(1)}, bf16[128,1024]{1,0:T(8,128)(2,1)}, u32[]{:S(2)}) copy-start(bf16[128,1024]{1,0:T(8,128)(2,1)} %get-tuple-element.9) | copy-start | bytes 786436
  100.2 1.0 %copy-start = (bf16[128,1024]{1,0:T(8,128)(2,1)S(1)}, bf16[128,1024]{1,0:T(8,128)(2,1)}, u32[]{:S(2)}) copy-start(bf16[128,1024]{1,0:T(8,128)(2,1)} %get-tuple-element.10) | copy-start | bytes 786436

commit v8 on v7

--- a/solution.py
+++ b/solution.py
@@ -224,6 +224,8 @@
         w_share(dx, yl, KS1).start()
     project_side([0], 1 - yl, KS2)
     project_side(x_near, yl, KS1)
+    for dx in x_near:
+        cot_along(dx).start()
     for dx in x_far:
         for part in range(2):
             w_arrive(dx, part)
@@ -231,7 +233,6 @@
     for dx in x_near:
         w_arrive_across(dx)
     for dx in x_near:
-        cot_along(dx).start()
         tok_along(dx, tm, KT1).start()
     project_side(x_near, 1 - yl, KS2)
     project_side(x_far, yl, KS1)

time: 102 us -> 101 us (level)
  Pallas kernels: 96.7 us -> 95.5 us
    pallas_call x1, Pallas kernels: 96.7 us -> 95.5 us  [shards(): pl.pallas_call(functools.partial(kernel, n_d, n_z, n_t, depth), out_shape...]
where the time goes in v8:
time: 101 us
  Pallas kernels  95.5 us (95%)
  local copies, waits for them, and re-layouts  3.96 us (4%)
  between operations  1.3 us (1%)
    pallas_call x1, Pallas kernels, shards(): pl.pallas_call(functools.partial(kernel, n_d, n_z, n_t, depth), out_shape...  95.5 us
    slice x1, local copies, waits for them, and re-layouts, shards(): grads[depth:lanes]  2.21 us

profile of v8, /device:TPU:1, one launch (start us, length us, event | category | flops | bytes accessed | tf_op | source)
XLA Modules:
  0.0 100.8 jit_solution(13222238087302796192)
XLA Ops:
  1.3 95.5 %shard_map.127 = (bf16[128,1024]{1,0:T(8,128)(2,1)}, bf16[128,1024]{1,0:T(8,128)(2,1)}, f32[256,1024]{1,0:T(8,128)}) custom-call(bf16[128,1024]{1,0:T(8,128)(2,1)} %bitcast.15, bf16[128,1024]{1,0:T(8,128)(2,1)} %bitcast.16, bf16[64,1024]{1,0:T(8,128)(2,1)} %bitcast.17, bf16[64,1024]{1,0:T(8,128)(2,1)} %bitcast.18, bf16[64,1024]{1,0:T(8,128)(2,1)} %bitcast.19, ...), custom_call_target="tpu_custom_call" | custom-call | flops 3000000000 | bytes 8000000 | tf_op jit(solution)/shard_map/pallas_call | solution.py:547
  96.8 0.0 copy-start.1
  96.8 2.2 %fusion = (f32[64,1024]{1,0:T(8,128)}, f32[1024,64]{0,1:T(8,128)}, f32[1024,64]{0,1:T(8,128)}, f32[1024,64]{0,1:T(8,128)}) fusion(f32[256,1024]{1,0:T(8,128)} %get-tuple-element.11), kind=kLoop, calls=%fused_computation.3 | loop fusion | bytes 2097152 | tf_op jit(solution)/shard_map/slice | solution.py:597
  99.1 0.0 copy-done.1
  99.1 0.0 copy-start
  99.1 0.7 copy.17
  99.8 0.3 copy-done
  100.1 0.7 copy.18
Async XLA Ops:
  96.8 2.2 %copy-start.1 = (bf16[128,1024]{1,0:T(8,128)(2,1)S(1)}, bf16[128,1024]{1,0:T(8,128)(2,1)}, u32[]{:S(2)}) copy-start(bf16[128,1024]{1,0:T(8,128)(2,1)} %get-tuple-element.9) | copy-start | bytes 786436
  99.1 1.0 %copy-start = (bf16[128,1024]{1,0:T(8,128)(2,1)S(1)}, bf16[128,1024]{1,0:T(8,128)(2,1)}, u32[]{:S(2)}) copy-start(bf16[128,1024]{1,0:T(8,128)(2,1)} %get-tuple-element.10) | copy-start | bytes 786436
